TPU v7x, 512 devices: a whole 4x8x8 slice. The times are simulated.
512 devices in a mesh: segment: 4 (over y_hi), tile: 16 (over z, y_lo), frame: 8 (over x, core).
Axes of the slice: x: 4, y: 8 (y_hi: 4, y_lo: 2; y = y_hi * 2 + y_lo), z: 8, core: 2. Of those that a mesh axis runs over, the one named last changes fastest.
Arguments:
- corrupted_clip: bfloat16 [4, 16, 128, 64, 128], P('segment', 'frame', 'tile'), may hold values from -6 to 6
- completed_clip_upsized: bfloat16 [4, 16, 128, 64, 128], P('segment', 'frame', 'tile'), may hold values from -6 to 6
- conditioning_frame: int32 [4, 16], P('segment', 'frame'), may hold values from 0 to 15
- inbound_kernel_matrix: bfloat16 [4, 3, 3, 256, 128], P('segment'), may hold values from -0.125 to 0.125
- skip_kernel_matrix: bfloat16 [4, 3, 3, 128, 128], P('segment'), may hold values from -0.1875 to 0.1875
- projection_matrices: bfloat16 [4, 4, 128, 128], P('segment'), may hold values from -0.5 to 0.5
- branch_logit_factor: float32 [4, 2], P('segment'), may hold values from 1 to 600
- expand_matrix: bfloat16 [4, 128, 512], P('segment'), may hold values from -0.5 to 0.5
- contract_matrix: bfloat16 [4, 512, 128], P('segment'), may hold values from -0.25 to 0.25
- outbound_kernel_matrix: bfloat16 [4, 3, 3, 128, 128], P('segment'), may hold values from -0.1875 to 0.1875
- update_factors: float32 [4, 2], P('segment'), may hold values from 0.2 to 1
Outputs:
- denoised_clip: bfloat16 [4, 16, 128, 64, 128], P('segment', 'frame', 'tile')
- predicted_perturbation: bfloat16 [4, 16, 128, 64, 128], P('segment', 'frame', 'tile')
All inputs are finite; a program needn't handle non-finite values.
Results may differ from a plain program's by a relative error of at most 0.014.
Values may be sent and summed in bfloat16 or wider, within the bound.
A program may use at most 64 MiB of HBM per device.

v0:
```python
import jax
import jax.numpy as jnp
from jax import lax
from jax.sharding import PartitionSpec as P


def extended(x, sides, width):
    for axis, dim in sides:
        size, length = (lax.axis_size(axis), x.shape[dim])
        up = [(i, (i + 1) % size) for i in range(size - 1)]
        down = [(j, i) for i, j in up]
        last = lax.slice_in_dim(x, length - width, length, axis=dim)
        leading = lax.slice_in_dim(x, 0, width, axis=dim)
        before = lax.ppermute(last, axis, up)
        after = lax.ppermute(leading, axis, down)
        x = jnp.concatenate([before, x, after], axis=dim)
    return x


def from_behind(block, axis, distance):
    devices = range(lax.axis_size(axis))
    route = [(i - distance, i) for i in devices if i - distance in devices]
    return lax.ppermute(block, axis, route)


def conv_rows(feature, kernel):
    rows = feature.shape[1]
    width = feature.shape[2]
    padded = extended(feature, (("tile", 1),), 1)
    padded = jnp.pad(padded, ((0, 0), (0, 0), (1, 1), (0, 0)))
    total = jnp.zeros(feature.shape[:3] + (kernel.shape[3],), jnp.float32)
    for row_off in range(3):
        for col_off in range(3):
            window_part = padded[:, row_off : row_off + rows, col_off : col_off + width]
            total = total + jnp.einsum(
                "frwc,cd->frwd",
                window_part,
                kernel[row_off, col_off],
                preferred_element_type=jnp.float32,
            )
    return total


def normed(value):
    return value * lax.rsqrt(jnp.mean(value * value, axis=-1, keepdims=True) + 1e-06)


def project(feature, weight):
    return jnp.einsum("frwc,cd->frwd", feature, weight, preferred_element_type=jnp.float32)


def head_scores(query, keys, logit_factor):
    return (
        jnp.einsum("fphd,gphd->fgph", query, keys, preferred_element_type=jnp.float32)
        * logit_factor
    )


def local(
    corrupted_clip,
    completed_clip_upsized,
    conditioning_frame,
    inbound_kernel_matrix,
    skip_kernel_matrix,
    projection_matrices,
    branch_logit_factor,
    expand_matrix,
    contract_matrix,
    outbound_kernel_matrix,
    update_factors,
):
    current = corrupted_clip[0]
    frames_dev, rows, width, chans = current.shape
    branch_total = branch_logit_factor.shape[1]
    per_branch_width = chans // branch_total
    logit_factor = branch_logit_factor[0] / per_branch_width
    clip = completed_clip_upsized[0]
    picks = conditioning_frame[0]
    lowered = from_behind(clip, "segment", 1)
    piece = lax.all_gather(lowered, "frame", axis=0, tiled=True)
    count = piece.shape[0]
    onehot = (picks[:, None] == jnp.arange(count, dtype=jnp.int32)[None, :]).astype(jnp.bfloat16)
    conditioning_source = jnp.einsum(
        "fg,grwc->frwc", onehot, piece, preferred_element_type=jnp.float32
    ).astype(jnp.bfloat16)
    joined = jnp.concatenate([current, conditioning_source], axis=-1)
    h1 = jax.nn.silu(conv_rows(joined, inbound_kernel_matrix[0])).astype(jnp.bfloat16)
    a = h1.astype(jnp.float32) + conv_rows(h1, skip_kernel_matrix[0])
    u = normed(a).astype(jnp.bfloat16)
    proj = projection_matrices[0]
    query = project(u, proj[0]).reshape(frames_dev, rows, width, branch_total, per_branch_width)
    keys = project(u, proj[1]).reshape(frames_dev, rows, width, branch_total, per_branch_width)
    qn = normed(query).astype(jnp.bfloat16).reshape(frames_dev, rows, width, chans)
    kn = normed(keys).astype(jnp.bfloat16).reshape(frames_dev, rows, width, chans)
    values = project(u, proj[2]).astype(jnp.bfloat16)
    pixels = rows * width
    qh = qn.reshape(frames_dev, pixels, branch_total, per_branch_width)
    start_peak = jnp.full((frames_dev, pixels, branch_total), -1e30, jnp.float32)
    pieces = (
        lax.all_gather(kn, "frame", axis=0, tiled=True),
        lax.all_gather(values, "frame", axis=0, tiled=True),
    )
    peak = start_peak
    count = pieces[0].shape[0]
    kh = pieces[0].reshape(count, pixels, branch_total, per_branch_width)
    vh = pieces[1].reshape(count, pixels, branch_total, per_branch_width)
    scores = head_scores(qh, kh, logit_factor)
    fresh = jnp.maximum(peak, jnp.max(scores, axis=1))
    raw = jnp.exp(scores - fresh[:, None])
    total = jnp.sum(raw, axis=1)
    acc = jnp.einsum(
        "fgph,gphd->fphd", raw.astype(jnp.bfloat16), vh, preferred_element_type=jnp.float32
    )
    peak, total, acc = (fresh, total, acc)
    attended = (acc / total[..., None]).astype(jnp.bfloat16).reshape(frames_dev, rows, width, chans)
    b = a + project(attended, proj[3])
    r = normed(b).astype(jnp.bfloat16)
    m = jax.nn.silu(project(r, expand_matrix[0])).astype(jnp.bfloat16)
    c = (b + project(m, contract_matrix[0])).astype(jnp.bfloat16)
    eps = conv_rows(c, outbound_kernel_matrix[0])
    denoised_clip = update_factors[0, 0] * current.astype(jnp.float32) - update_factors[0, 1] * eps
    return (denoised_clip.astype(jnp.bfloat16)[None], eps.astype(jnp.bfloat16)[None])


def solution(mesh):
    in_specs = (
        P("segment", "frame", "tile", None, None),
        P("segment", "frame", "tile", None, None),
        P("segment", "frame"),
        P("segment", None, None, None, None),
        P("segment", None, None, None, None),
        P("segment", None, None, None),
        P("segment", None),
        P("segment", None, None),
        P("segment", None, None),
        P("segment", None, None, None, None),
        P("segment", None),
    )
    out_specs = (
        P("segment", "frame", "tile", None, None),
        P("segment", "frame", "tile", None, None),
    )
    return jax.shard_map(local, mesh=mesh, in_specs=in_specs, out_specs=out_specs, check_vma=False)
```

profile of v0, /device:TPU:233, one launch (start us, length us, event | category | flops | bytes accessed | tf_op | source)
XLA Modules:
  0.0 194.4 jit_solution(3893484889308535267)
XLA Ops:
  7.2 2.6 %collective-permute-start = (bf16[2,8,64,128]{3,2,1,0:T(8,128)(2,1)}, bf16[2,8,64,128]{3,2,1,0:T(8,128)(2,1)S(1)}, u32[]{:S(2)}, u32[]{:S(2)}) collective-permute-start(bf16[2,8,64,128]{3,2,1,0:T(8,128)(2,1)} %bitcast.332), channel_id=1, source_target_pairs={{0,128},{128,256},{256,384},{1,129},{129,257},{257,385},{2,130},{1... | collective-permute-start | bytes 786440 | tf_op jit(solution)/shard_map/ppermute | solution.py:23
  9.8 13.5 %collective-permute-done = bf16[2,8,64,128]{3,2,1,0:T(8,128)(2,1)S(1)} collective-permute-done((bf16[2,8,64,128]{3,2,1,0:T(8,128)(2,1)}, bf16[2,8,64,128]{3,2,1,0:T(8,128)(2,1)S(1)}, u32[]{:S(2)}, u32[]{:S(2)}) %collective-permute-start) | collective-permute-done | bytes 262176 | tf_op jit(solution)/shard_map/ppermute | solution.py:23
  24.1 34.9 %all-gather.4.cloned.1.call-done = bf16[16,8,64,128]{3,2,1,0:T(8,128)(2,1)} async-done(((bf16[2,8,64,128]{3,2,1,0:T(8,128)(2,1)}), bf16[16,8,64,128]{3,2,1,0:T(8,128)(2,1)}) %all-gather.4.cloned.1.call-update) | async-done | bytes 2097168 | tf_op jit(solution)/shard_map/all_gather | solution.py:80
  59.0 3.0 %fusion.4 = bf16[2,8,64,128]{3,0,2,1:T(2,128)(2,1)S(1)} fusion(bf16[16,8,64,128]{3,2,1,0:T(8,128)(2,1)} %all-gather.4.cloned.1.call-done, s32[2]{0:T(128)} %bitcast.331), kind=kOutput, calls=%fused_computation.6 | convolution fusion | flops 4194336 | bytes 2359304 | tf_op jit(solution)/shard_map/fg,grwc->frwc/dot_general | solution.py:83
  62.1 5.4 %collective-permute-start.1 = (bf16[2,1,64,256]{3,2,1,0:T(8,128)(2,1)S(1)}, bf16[2,1,64,256]{3,2,1,0:T(8,128)(2,1)S(1)}, u32[]{:S(2)}, u32[]{:S(2)}) collective-permute-start(bf16[2,1,64,256]{3,2,1,0:T(8,128)(2,1)S(1)} %get-tuple-element.10), channel_id=1, source_target_pairs={{0,8},{8,16},{16,24},{24,32},{32,40},{40,48},{48,56},{56,64},{64,7... | collective-permute-start | bytes 196616 | tf_op jit(solution)/shard_map/ppermute | solution.py:14
  67.4 1.9 collective-permute-start.2
  69.4 5.2 %collective-permute-done.2 = bf16[2,1,64,256]{3,2,1,0:T(8,128)(2,1)S(1)} collective-permute-done((bf16[2,1,64,256]{3,2,1,0:T(8,128)(2,1)S(1)}, bf16[2,1,64,256]{3,2,1,0:T(8,128)(2,1)S(1)}, u32[]{:S(2)}, u32[]{:S(2)}) %collective-permute-start.2) | collective-permute-done | bytes 65568 | tf_op jit(solution)/shard_map/ppermute | solution.py:15
  77.8 1.9 collective-permute-start.3
  79.7 3.4 %collective-permute-start.4 = (bf16[2,1,64,128]{3,2,1,0:T(8,128)(2,1)S(1)}, bf16[2,1,64,128]{3,2,1,0:T(8,128)(2,1)S(1)}, u32[]{:S(2)}, u32[]{:S(2)}) collective-permute-start(bf16[2,1,64,128]{3,2,1,0:T(8,128)(2,1)S(1)} %get-tuple-element.15), channel_id=1, source_target_pairs={{8,0},{16,8},{24,16},{32,24},{40,32},{48,40},{56,48},{64,56},{72,6... | collective-permute-start | bytes 98312 | tf_op jit(solution)/shard_map/ppermute | solution.py:15
  83.2 3.2 %collective-permute-done.4 = bf16[2,1,64,128]{3,2,1,0:T(8,128)(2,1)S(1)} collective-permute-done((bf16[2,1,64,128]{3,2,1,0:T(8,128)(2,1)S(1)}, bf16[2,1,64,128]{3,2,1,0:T(8,128)(2,1)S(1)}, u32[]{:S(2)}, u32[]{:S(2)}) %collective-permute-start.4) | collective-permute-done | bytes 32800 | tf_op jit(solution)/shard_map/ppermute | solution.py:15
  92.8 28.1 %all-gather.8.cloned.1.call-done = bf16[16,8,64,128]{3,2,1,0:T(8,128)(2,1)} async-done(((bf16[2,8,64,128]{3,2,1,0:T(8,128)(2,1)}), bf16[16,8,64,128]{3,2,1,0:T(8,128)(2,1)}) %all-gather.8.cloned.1.call-update) | async-done | bytes 2097168 | tf_op jit(solution)/shard_map/all_gather | solution.py:100
  120.9 8.2 %reshape.112 = bf16[16,512,2,64]{3,2,1,0:T(2,128)(2,1)} reshape(bf16[16,8,64,128]{3,2,1,0:T(8,128)(2,1)} %all-gather.8.cloned.1.call-done) | data formatting | bytes 4194304 | tf_op jit(solution)/shard_map/reshape | solution.py:105
  129.1 5.7 %fusion.122 = (f32[2,512,2]{0,2,1:T(2,128)S(1)}, f32[2,16,512,2]{1,0,3,2:T(2,128)S(1)}) fusion(f32[2]{0:T(128)S(1)} %multiply_bitcast_fusion, bf16[2,512,2,64]{3,0,2,1:T(2,128)(2,1)S(1)} %bitcast.301, bf16[16,512,2,64]{3,2,1,0:T(2,128)(2,1)} %reshape.112), kind=kOutput, calls=%fused_computation.193 | convolution fusion | flops 4257792 | bytes 2498568 | tf_op jit(solution)/shard_map/fphd,gphd->fgph/dot_general | solution.py:54
  135.0 14.3 %fusion.40 = f32[2,512,2]{0,2,1:T(2,128)S(1)} fusion(f32[2,16,512,2]{1,0,3,2:T(2,128)S(1)} %get-tuple-element.27, f32[2,512,2]{0,2,1:T(2,128)S(1)} %broadcast_maximum_fusion), kind=kLoop, calls=%fused_computation.68 | loop fusion | flops 63488 | bytes 147456 | tf_op jit(solution)/shard_map/reduce_sum | solution.py:110
  149.5 4.9 %all-gather.6.cloned.1.call-done = bf16[16,8,64,128]{3,2,1,0:T(8,128)(2,1)} async-done(((bf16[2,8,64,128]{3,2,1,0:T(8,128)(2,1)}), bf16[16,8,64,128]{3,2,1,0:T(8,128)(2,1)}) %all-gather.6.cloned.1.call-update) | async-done | bytes 2097168 | tf_op jit(solution)/shard_map/all_gather | solution.py:101
  154.5 8.2 %reshape.111 = bf16[16,512,2,64]{3,2,1,0:T(2,128)(2,1)} reshape(bf16[16,8,64,128]{3,2,1,0:T(8,128)(2,1)} %all-gather.6.cloned.1.call-done) | data formatting | bytes 4194304 | tf_op jit(solution)/shard_map/reshape | solution.py:106
  162.7 5.3 %fusion.2 = f32[512,2,64,2]{2,3,1,0:T(2,128)S(1)} fusion(bf16[16,512,2,64]{3,2,1,0:T(2,128)(2,1)} %reshape.111, f32[2,16,512,2]{1,0,3,2:T(2,128)S(1)} %get-tuple-element.27, f32[2,512,2]{0,2,1:T(2,128)S(1)} %broadcast_maximum_fusion), kind=kOutput, calls=%fused_computation.2 | convolution fusion | flops 4259840 | bytes 2760704 | tf_op jit(solution)/shard_map/fgph,gphd->fphd/dot_general | solution.py:111
  167.9 1.0 copy.127
  169.3 1.2 multiply_reduce_fusion.2
  170.5 0.9 fusion.22
  171.5 5.4 %collective-permute-start.5 = (bf16[2,1,64,128]{3,2,1,0:T(8,128)(2,1)S(1)}, bf16[2,1,64,128]{3,2,1,0:T(8,128)(2,1)S(1)}, u32[]{:S(2)}, u32[]{:S(2)}) collective-permute-start(bf16[2,1,64,128]{3,2,1,0:T(8,128)(2,1)S(1)} %get-tuple-element.12), channel_id=1, source_target_pairs={{0,8},{8,16},{16,24},{24,32},{32,40},{40,48},{48,56},{56,64},{64,7... | collective-permute-start | bytes 98312 | tf_op jit(solution)/shard_map/ppermute | solution.py:14
  176.9 1.9 collective-permute-start.6
  179.4 4.2 %collective-permute-done.6 = bf16[2,1,64,128]{3,2,1,0:T(8,128)(2,1)S(1)} collective-permute-done((bf16[2,1,64,128]{3,2,1,0:T(8,128)(2,1)S(1)}, bf16[2,1,64,128]{3,2,1,0:T(8,128)(2,1)S(1)}, u32[]{:S(2)}, u32[]{:S(2)}) %collective-permute-start.6) | collective-permute-done | bytes 32800 | tf_op jit(solution)/shard_map/ppermute | solution.py:15
  185.5 2.3 %convert_bitcast_fusion = (bf16[1,2,8,64,128]{4,3,2,1,0:T(8,128)(2,1)}, bf16[1,2,8,64,128]{4,3,2,1,0:T(8,128)(2,1)}) fusion(f32[]{:T(128)} %bitcast.2, bf16[1,2,8,64,128]{4,3,2,1,0:T(8,128)(2,1)S(1)} %copy-done.1, f32[]{:T(128)} %bitcast, f32[2,8,64,128]{3,2,1,0:T(8,128)S(1)} %fusion.80, f32[2,8,64,128]{3,2,1,0:T(8,128)S(1)} %fusion.75, ...), kind=kOutput, calls=%fused_computation.133 | convolution fusion | flops 34734080 | bytes 2654216 | tf_op jit(solution)/shard_map/frwc,cd->frwd/dot_general | solution.py:35
  (83 shorter events, 13.5 us)
Async XLA Ops:
  7.2 163.3 %copy-start = (bf16[1,512,128]{2,1,0:T(8,128)(2,1)S(1)}, bf16[1,512,128]{2,1,0:T(8,128)(2,1)}, u32[]{:S(2)}) copy-start(bf16[1,512,128]{2,1,0:T(8,128)(2,1)} %param.19) | copy-start | bytes 393220
  7.2 54.8 %copy-start.1 = (bf16[1,2,8,64,128]{4,3,2,1,0:T(8,128)(2,1)S(1)}, bf16[1,2,8,64,128]{4,3,2,1,0:T(8,128)(2,1)}, u32[]{:S(2)}) copy-start(bf16[1,2,8,64,128]{4,3,2,1,0:T(8,128)(2,1)} %param.11) | copy-start | bytes 786436
  7.2 51.8 %all-gather.4.cloned.1.call-start = ((), (), s32[]{:S(2)}) async-start(), calls=%async_computation | async-start | bytes 2359296 | tf_op jit(solution)/shard_map/all_gather | solution.py:80
  7.2 16.1 %collective-permute-start = (bf16[2,8,64,128]{3,2,1,0:T(8,128)(2,1)}, bf16[2,8,64,128]{3,2,1,0:T(8,128)(2,1)S(1)}, u32[]{:S(2)}, u32[]{:S(2)}) collective-permute-start(bf16[2,8,64,128]{3,2,1,0:T(8,128)(2,1)} %bitcast.332), channel_id=1, source_target_pairs={{0,128},{128,256},{256,384},{1,129},{129,257},{257,385},{2,130},{1... | collective-permute-start | bytes 786440 | tf_op jit(solution)/shard_map/ppermute | solution.py:23
  23.3 0.7 copy-start.4
  24.1 96.8 %all-gather.8.cloned.1.call-start = ((), (), s32[]{:S(2)}) async-start(), calls=%async_computation.2 | async-start | bytes 2359296 | tf_op jit(solution)/shard_map/all_gather | solution.py:100
  59.0 15.9 %copy-start.5 = (bf16[1,3,3,256,128]{4,3,2,1,0:T(8,128)(2,1)S(1)}, bf16[1,3,3,256,128]{4,3,2,1,0:T(8,128)(2,1)}, u32[]{:S(2)}) copy-start(bf16[1,3,3,256,128]{4,3,2,1,0:T(8,128)(2,1)} %param.14) | copy-start | bytes 1769476
  62.1 7.3 %collective-permute-start.1 = (bf16[2,1,64,256]{3,2,1,0:T(8,128)(2,1)S(1)}, bf16[2,1,64,256]{3,2,1,0:T(8,128)(2,1)S(1)}, u32[]{:S(2)}, u32[]{:S(2)}) collective-permute-start(bf16[2,1,64,256]{3,2,1,0:T(8,128)(2,1)S(1)} %get-tuple-element.10), channel_id=1, source_target_pairs={{0,8},{8,16},{16,24},{24,32},{32,40},{40,48},{48,56},{56,64},{64,7... | collective-permute-start | bytes 196616 | tf_op jit(solution)/shard_map/ppermute | solution.py:14
  67.4 7.1 %collective-permute-start.2 = (bf16[2,1,64,256]{3,2,1,0:T(8,128)(2,1)S(1)}, bf16[2,1,64,256]{3,2,1,0:T(8,128)(2,1)S(1)}, u32[]{:S(2)}, u32[]{:S(2)}) collective-permute-start(bf16[2,1,64,256]{3,2,1,0:T(8,128)(2,1)S(1)} %get-tuple-element.11), channel_id=1, source_target_pairs={{8,0},{16,8},{24,16},{32,24},{40,32},{48,40},{56,48},{64,56},{72,6... | collective-permute-start | bytes 196616 | tf_op jit(solution)/shard_map/ppermute | solution.py:15
  77.4 5.7 %copy-start.6 = (bf16[1,4,128,128]{3,2,1,0:T(8,128)(2,1)S(1)}, bf16[1,4,128,128]{3,2,1,0:T(8,128)(2,1)}, u32[]{:S(2)}) copy-start(bf16[1,4,128,128]{3,2,1,0:T(8,128)(2,1)} %param.16) | copy-start | bytes 393220
  77.4 9.2 %copy-start.3 = (bf16[1,3,3,128,128]{4,3,2,1,0:T(8,128)(2,1)S(1)}, bf16[1,3,3,128,128]{4,3,2,1,0:T(8,128)(2,1)}, u32[]{:S(2)}) copy-start(bf16[1,3,3,128,128]{4,3,2,1,0:T(8,128)(2,1)} %param.15) | copy-start | bytes 884740
  77.8 5.4 %collective-permute-start.3 = (bf16[2,1,64,128]{3,2,1,0:T(8,128)(2,1)S(1)}, bf16[2,1,64,128]{3,2,1,0:T(8,128)(2,1)S(1)}, u32[]{:S(2)}, u32[]{:S(2)}) collective-permute-start(bf16[2,1,64,128]{3,2,1,0:T(8,128)(2,1)S(1)} %get-tuple-element.14), channel_id=1, source_target_pairs={{0,8},{8,16},{16,24},{24,32},{32,40},{40,48},{48,56},{56,64},{64,7... | collective-permute-start | bytes 98312 | tf_op jit(solution)/shard_map/ppermute | solution.py:14
  79.7 6.8 %collective-permute-start.4 = (bf16[2,1,64,128]{3,2,1,0:T(8,128)(2,1)S(1)}, bf16[2,1,64,128]{3,2,1,0:T(8,128)(2,1)S(1)}, u32[]{:S(2)}, u32[]{:S(2)}) collective-permute-start(bf16[2,1,64,128]{3,2,1,0:T(8,128)(2,1)S(1)} %get-tuple-element.15), channel_id=1, source_target_pairs={{8,0},{16,8},{24,16},{32,24},{40,32},{48,40},{56,48},{64,56},{72,6... | collective-permute-start | bytes 98312 | tf_op jit(solution)/shard_map/ppermute | solution.py:15
  89.3 2.2 %copy-start.9 = (f32[1,2]{1,0:T(1,128)S(1)}, f32[1,2]{1,0:T(1,128)}, u32[]{:S(2)}) copy-start(f32[1,2]{1,0:T(1,128)} %param.17) | copy-start | bytes 28
  90.4 64.0 %all-gather.6.cloned.1.call-start = ((), (), s32[]{:S(2)}) async-start(), calls=%async_computation.1 | async-start | bytes 2359296 | tf_op jit(solution)/shard_map/all_gather | solution.py:101
  167.9 2.6 %copy-start.8 = (bf16[1,128,512]{2,1,0:T(8,128)(2,1)S(1)}, bf16[1,128,512]{2,1,0:T(8,128)(2,1)}, u32[]{:S(2)}) copy-start(bf16[1,128,512]{2,1,0:T(8,128)(2,1)} %param.18) | copy-start | bytes 393220
  170.5 8.3 %copy-start.7 = (f32[1,2]{1,0:T(1,128)S(1)}, f32[1,2]{1,0:T(1,128)}, u32[]{:S(2)}) copy-start(f32[1,2]{1,0:T(1,128)} %param.21) | copy-start | bytes 28
  170.5 13.2 %copy-start.2 = (bf16[1,3,3,128,128]{4,3,2,1,0:T(8,128)(2,1)S(1)}, bf16[1,3,3,128,128]{4,3,2,1,0:T(8,128)(2,1)}, u32[]{:S(2)}) copy-start(bf16[1,3,3,128,128]{4,3,2,1,0:T(8,128)(2,1)} %param.20) | copy-start | bytes 884740
  171.5 7.9 %collective-permute-start.5 = (bf16[2,1,64,128]{3,2,1,0:T(8,128)(2,1)S(1)}, bf16[2,1,64,128]{3,2,1,0:T(8,128)(2,1)S(1)}, u32[]{:S(2)}, u32[]{:S(2)}) collective-permute-start(bf16[2,1,64,128]{3,2,1,0:T(8,128)(2,1)S(1)} %get-tuple-element.12), channel_id=1, source_target_pairs={{0,8},{8,16},{16,24},{24,32},{32,40},{40,48},{48,56},{56,64},{64,7... | collective-permute-start | bytes 98312 | tf_op jit(solution)/shard_map/ppermute | solution.py:14
  176.9 6.8 %collective-permute-start.6 = (bf16[2,1,64,128]{3,2,1,0:T(8,128)(2,1)S(1)}, bf16[2,1,64,128]{3,2,1,0:T(8,128)(2,1)S(1)}, u32[]{:S(2)}, u32[]{:S(2)}) collective-permute-start(bf16[2,1,64,128]{3,2,1,0:T(8,128)(2,1)S(1)} %get-tuple-element.13), channel_id=1, source_target_pairs={{8,0},{16,8},{24,16},{32,24},{40,32},{48,40},{56,48},{64,56},{72,6... | collective-permute-start | bytes 98312 | tf_op jit(solution)/shard_map/ppermute | solution.py:15
Sparse Core Ops, SparseCore 0:
  24.2 34.7 all-gather.3
  90.6 30.2 all-gather.7
  123.6 30.8 all-gather.5
where the time goes:
time: 196 us; the launch traced here: 194 us
  waiting for transfers between devices  94.2 us (48%)
  matrix products  26.6 us (14%)
  starting transfers between devices  22.5 us (11%)
  local copies, waits for them, and re-layouts  21 us (11%)
  other arithmetic  15.8 us (8%)
  between operations  14.3 us (7%)
    all_gather x1, waiting for transfers between devices, local(): piece = lax.all_gather(lowered, 'frame', axis=0, tiled=True)  34.9 us
    all_gather x1, waiting for transfers between devices, local(): lax.all_gather(kn, 'frame', axis=0, tiled=True)  28.1 us
    reduce_sum x1, other arithmetic, local(): total = jnp.sum(raw, axis=1)  14.3 us
    ppermute x1, waiting for transfers between devices, from_behind(): return lax.ppermute(block, axis, route)  13.5 us
    ppermute x3, waiting for transfers between devices, extended(): after = lax.ppermute(leading, axis, down)  12.7 us
    ppermute x3, starting transfers between devices, extended(): before = lax.ppermute(last, axis, up)  12.6 us
    dot_general x27, matrix products, conv_rows(): jnp.einsum('frwc,cd->frwd', window_part, kernel[row_off, col_off], prefer...  8.82 us
    reshape x1, local copies, waits for them, and re-layouts, local(): kh = pieces[0].reshape(count, pixels, branch_total, per_branch_width)  8.2 us
  transfers between devices with their start and end apart: 10, of which 7 were waited for; matrix products, arithmetic and copies ran while one was open for 16% of the time, Pallas kernels for 0%

commit v1 on v0

v1 whole, which is shorter than its diff:
```python
import functools

import jax
import jax.numpy as jnp
from jax import lax
from jax.experimental import pallas as pl
from jax.experimental.pallas import tpu as pltpu
from jax.sharding import PartitionSpec as P

MESH = pl.DeviceIdType.MESH
BF = jnp.bfloat16
F32 = jnp.float32
PR, PC, NF, CH = 4, 16, 16, 128
DIRS = [(-1, 0), (1, 0), (0, -1), (0, 1), (-1, -1), (-1, 1), (1, -1), (1, 1)]
SRC_ROWS = {-1: slice(1, 2), 1: slice(PR, PR + 1), 0: slice(1, PR + 1)}
DST_ROWS = {-1: slice(PR + 1, PR + 2), 1: slice(0, 1), 0: slice(1, PR + 1)}
SRC_COLS = {-1: slice(1, 2), 1: slice(PC, PC + 1), 0: slice(1, PC + 1)}
DST_COLS = {-1: slice(PC + 1, PC + 2), 1: slice(0, 1), 0: slice(1, PC + 1)}


def dot(a, b):
    return jnp.dot(a, b, preferred_element_type=F32)


def lane_sums(v, ones):
    hi = v.astype(BF)
    lo = (v - hi.astype(F32)).astype(BF)
    return dot(jnp.concatenate([hi, lo], axis=1), jnp.concatenate([ones, ones], axis=0))


def silu(v):
    return v / (1.0 + jnp.exp(-v))


def kernel(
    x_hbm, clip_hbm, picks, w_in, w_mid, proj, factors, w_up, w_dn, w_out, coefs,
    den_out, eps_out,
    raw_n, raw_c, xn, xc, hb, cb, acc, res, pk, send_e, eo, xv, dv,
    v_in_n, v_in_c, v_mid, v_qkv, v_o, v_up, v_dn, v_out,
    s_w, s_pk, r_pk, s_c, r_c, s_n, r_n, s_h, r_h, s_e, r_e, s_fin,
):
    s = lax.axis_index("segment")
    t = lax.axis_index("tile")
    d = lax.axis_index("frame")
    i, j = lax.rem(d, 2), lax.div(d, 2)
    big_row = 2 * t + i
    last_row = 2 * lax.axis_size("tile") - 1

    weights = [
        (w_in.at[0, :, :, 0:CH, :], v_in_n),
        (x_hbm.at[0], xv),
        (w_in.at[0, :, :, CH : 2 * CH, :], v_in_c),
        (w_mid.at[0], v_mid),
        (proj.at[0, 0], v_qkv.at[:, 0:CH]),
        (proj.at[0, 1], v_qkv.at[:, CH : 2 * CH]),
        (proj.at[0, 2], v_qkv.at[:, 2 * CH : 3 * CH]),
        (proj.at[0, 3], v_o),
        (w_up.at[0], v_up),
        (w_dn.at[0], v_dn),
        (w_out.at[0], v_out),
    ]
    loads = [pltpu.make_async_copy(a, b, s_w.at[q]) for q, (a, b) in enumerate(weights)]

    def neighbour(step_row, step_col):
        row = lax.rem(big_row + step_row + last_row + 1, last_row + 1)
        col = lax.rem(j + step_col + 4, 4)
        return {"tile": lax.div(row, 2), "frame": 2 * col + lax.rem(row, 2)}

    def in_group(k):
        return lax.rem(d + k, 8)

    barrier = pltpu.get_barrier_semaphore()
    for k in range(8):
        for step in (1, 3):
            pl.semaphore_signal(
                barrier, inc=1, device_id={"segment": lax.rem(s + step, 4), "frame": in_group(k)}, device_id_type=MESH
            )
    for k in range(1, 8):
        pl.semaphore_signal(barrier, inc=1, device_id={"frame": in_group(k)}, device_id_type=MESH)
    for step in DIRS:
        pl.semaphore_signal(barrier, inc=1, device_id=neighbour(*step), device_id_type=MESH)
    for load in loads:
        load.start()
    pl.semaphore_wait(barrier, 16 + 7 + 8)

    def patch_of(ref, c):
        return ref.at[0, :, pl.ds(PR * lax.rem(c, 2), PR), pl.ds(pl.multiple_of(PC * lax.div(c, 2), PC), PC), :]

    clip_copies = [
        pltpu.make_async_remote_copy(
            src_ref=patch_of(clip_hbm, in_group(k)),
            dst_ref=raw_c.at[d],
            send_sem=s_c.at[k],
            recv_sem=r_c.at[k],
            device_id={"segment": lax.rem(s + 1, 4), "frame": in_group(k)},
            device_id_type=MESH,
        )
        for k in range(8)
    ]

    @pl.when(s < 3)
    def _():
        for copy in clip_copies:
            copy.start()

    frame_row = lax.broadcasted_iota(jnp.int32, (NF, CH), 0)
    pk[d] = jnp.where(frame_row == 2 * d, picks[0, 0], jnp.where(frame_row == 2 * d + 1, picks[0, 1], 0)).astype(F32)
    pick_copies, noisy_copies = [], []
    own_noisy = pltpu.make_async_copy(patch_of(x_hbm, d), raw_n.at[d], s_n.at[0])
    own_noisy.start()
    for k in range(1, 8):
        noisy_copies.append(
            pltpu.make_async_remote_copy(
                src_ref=patch_of(x_hbm, in_group(k)),
                dst_ref=raw_n.at[d],
                send_sem=s_n.at[k],
                recv_sem=r_n.at[k],
                device_id={"frame": in_group(k)},
                device_id_type=MESH,
            )
        )
        noisy_copies[-1].start()
    for k in range(1, 8):
        pick_copies.append(
            pltpu.make_async_remote_copy(
                src_ref=pk.at[d],
                dst_ref=pk.at[d],
                send_sem=s_pk.at[k],
                recv_sem=r_pk.at[k],
                device_id={"frame": in_group(k)},
                device_id_type=MESH,
            )
        )
        pick_copies[-1].start()

    r_i = lax.broadcasted_iota(jnp.int32, (256, 256), 0)
    c_i = lax.broadcasted_iota(jnp.int32, (256, 256), 1)
    r_hi, r_lo, c_hi, c_lo = r_i // 16, r_i % 16, c_i // 16, c_i % 16
    swap = jnp.where((r_hi == c_lo) & (r_lo == c_hi), 1.0, 0.0).astype(BF)

    def halo_copies(buf, n):
        copies = []
        for k, (dr, dc) in enumerate(DIRS):
            copies.append(
                pltpu.make_async_remote_copy(
                    src_ref=buf.at[SRC_ROWS[dr], SRC_COLS[dc]],
                    dst_ref=buf.at[DST_ROWS[dr], DST_COLS[dc]],
                    send_sem=s_h.at[n, k],
                    recv_sem=r_h.at[n, k],
                    device_id=neighbour(dr, dc),
                    device_id_type=MESH,
                )
            )
        return copies

    def halo_end(buf, copies):
        for copy in copies:
            copy.wait_recv()

        @pl.when(big_row == 0)
        def _():
            buf[0] = jnp.zeros((PC + 2, NF, CH), BF)

        @pl.when(big_row == last_row)
        def _():
            buf[PR + 1] = jnp.zeros((PC + 2, NF, CH), BF)

        @pl.when(j == 0)
        def _():
            buf[:, 0:1] = jnp.zeros((PR + 2, 1, NF, CH), BF)

        @pl.when(j == 3)
        def _():
            buf[:, PC + 1 : PC + 2] = jnp.zeros((PR + 2, 1, NF, CH), BF)

    def conv(buf, w, row, rows):
        n = rows * PC * NF
        parts = [
            buf[row + dr : row + dr + rows, dc : dc + PC].reshape(n, CH) for dr in range(3) for dc in range(3)
        ]
        return dot(jnp.concatenate(parts, axis=1), w[...].reshape(9 * CH, w.shape[3]))

    own_noisy.wait()
    for copy in noisy_copies:
        copy.wait_recv()
    for row in range(PR):
        xn[row + 1, 1 : PC + 1] = dot(swap, raw_n[:, :, row].reshape(256, CH)).astype(BF).reshape(PC, NF, CH)
    n_halo = halo_copies(xn, 0)
    for copy in n_halo:
        copy.start()
    loads[0].wait()
    halo_end(xn, n_halo)
    for row in range(0, PR, 2):
        acc[row * 256 : row * 256 + 512] = conv(xn, v_in_n, row, 2)

    for copy in pick_copies:
        copy.wait_recv()
    pick_rows = pk[0]
    for q in range(1, 8):
        pick_rows = pick_rows + pk[q]
    pick_rows = jnp.broadcast_to(pick_rows[None], (16, NF, CH)).reshape(256, CH)
    pick_rows = jnp.concatenate([pick_rows, pick_rows], axis=1)
    choose = jnp.where((r_hi == c_lo) & (pick_rows == c_hi.astype(F32)), 1.0, 0.0).astype(BF)

    @pl.when(s == 0)
    def _():
        raw_c[...] = jnp.zeros(raw_c.shape, BF)

    @pl.when(s > 0)
    def _():
        for copy in clip_copies:
            copy.wait_recv()

    for row in range(PR):
        xc[row + 1, 1 : PC + 1] = dot(choose, raw_c[:, :, row].reshape(256, CH)).astype(BF).reshape(PC, NF, CH)
    c_halo = halo_copies(xc, 1)
    for copy in c_halo:
        copy.start()
    for load in loads[1:]:
        load.wait()
    halo_end(xc, c_halo)
    for row in range(0, PR, 2):
        v = acc[row * 256 : row * 256 + 512] + conv(xc, v_in_c, row, 2)
        hb[row + 1 : row + 3, 1 : PC + 1] = silu(v).astype(BF).reshape(2, PC, NF, CH)
    h_halo = halo_copies(hb, 2)
    for copy in h_halo:
        copy.start()
    halo_end(hb, h_halo)

    lane_r = lax.broadcasted_iota(jnp.int32, (CH, CH), 0)
    lane_c = lax.broadcasted_iota(jnp.int32, (CH, CH), 1)
    ones = jnp.full((CH, CH), 1.0, BF)
    by_head = jnp.where(lane_r // 64 == lane_c // 64, 1.0, 0.0).astype(BF)
    first_head = lane_c < 64
    same_pixel = lane_r // 16 == lane_c // 16
    same_pixel = jnp.concatenate([same_pixel, same_pixel], axis=0)
    scale = jnp.concatenate(
        [jnp.full((CH, CH), factors[0, 0] * (1 / 64)), jnp.full((CH, CH), factors[0, 1] * (1 / 64))], axis=0
    )
    for row in range(0, PR, 2):
        skip = hb[row + 1 : row + 3, 1 : PC + 1].reshape(512, CH).astype(F32)
        res[row * 256 : row * 256 + 512] = skip + conv(hb, v_mid, row, 2)

    def per_row(row, carry):
        at = pl.multiple_of(row * 256, 256)
        a = res[pl.ds(at, 256)]
        u = (a * lax.rsqrt(lane_sums(a * a, ones) * (1 / 128) + 1e-6)).astype(BF)
        qkv = dot(u, v_qkv[...])
        q, k, v = qkv[:, 0:CH], qkv[:, CH : 2 * CH], qkv[:, 2 * CH : 3 * CH].astype(BF)
        qn = (q * lax.rsqrt(lane_sums(q * q, by_head) * (1 / 64) + 1e-6)).astype(BF)
        kn = (k * lax.rsqrt(lane_sums(k * k, by_head) * (1 / 64) + 1e-6)).astype(BF)
        parts = []
        for g in range(2):
            qg, kg, vg = (z[g * CH : (g + 1) * CH] for z in (qn, kn, v))
            zero = jnp.zeros((CH, CH), BF)
            both = jnp.concatenate([jnp.where(first_head, qg, zero), jnp.where(first_head, zero, qg)], axis=0)
            sc = lax.dot_general(both, kg, (((1,), (1,)), ((), ())), preferred_element_type=F32) * scale
            sc = jnp.where(same_pixel, sc, -1e30)
            e = jnp.exp(sc - jnp.max(sc, axis=1, keepdims=True))
            total = jnp.sum(e, axis=1, keepdims=True)
            o = dot(e.astype(BF), vg) / total
            parts.append(jnp.where(first_head, o[:CH], o[CH:]).astype(BF))
        b = a + dot(jnp.concatenate(parts, axis=0), v_o[...])
        r = (b * lax.rsqrt(lane_sums(b * b, ones) * (1 / 128) + 1e-6)).astype(BF)
        m = silu(dot(r, v_up[...])).astype(BF)
        c = (b + dot(m, v_dn[...])).astype(BF)
        cb[row + 1, 1 : PC + 1] = c.reshape(PC, NF, CH)
        return carry

    lax.fori_loop(0, PR, per_row, 0)
    last_halo = halo_copies(cb, 3)
    for copy in last_halo:
        copy.start()
    halo_end(cb, last_halo)
    eps = [conv(cb, v_out, row, 2) for row in (0, 2)]
    for row in range(PR):
        part = eps[row // 2][(row % 2) * 256 : (row % 2) * 256 + 256].astype(BF)
        send_e[:, row] = dot(swap, part).astype(BF).reshape(NF, PC, CH)
    mine = eo.at[:, pl.ds(PR * i, PR), pl.ds(pl.multiple_of(PC * j, PC), PC), :]
    own_eps = pltpu.make_async_copy(send_e.at[pl.ds(2 * d, 2)], mine, s_e.at[0])
    eps_copies = []
    for k in range(1, 8):
        eps_copies.append(
            pltpu.make_async_remote_copy(
                src_ref=send_e.at[pl.ds(2 * in_group(k), 2)],
                dst_ref=mine,
                send_sem=s_e.at[k],
                recv_sem=r_e.at[k],
                device_id={"frame": in_group(k)},
                device_id_type=MESH,
            )
        )
        eps_copies[-1].start()
    own_eps.start()
    own_eps.wait()
    for copy in eps_copies:
        copy.wait_recv()
    out_eps = pltpu.make_async_copy(eo, eps_out.at[0], s_fin.at[0])
    out_eps.start()
    dv[...] = (coefs[0, 0] * xv[...].astype(F32) - coefs[0, 1] * eo[...].astype(F32)).astype(BF)
    out_den = pltpu.make_async_copy(dv, den_out.at[0], s_fin.at[1])
    out_den.start()
    for copy in pick_copies + noisy_copies + n_halo + c_halo + h_halo + last_halo + eps_copies:
        copy.wait_send()

    @pl.when(s < 3)
    def _():
        for copy in clip_copies:
            copy.wait_send()

    out_eps.wait()
    out_den.wait()


def local(x, clip, picks, w_in, w_mid, proj, factors, w_up, w_dn, w_out, coefs):
    hbm = pl.BlockSpec(memory_space=pl.ANY)
    smem = pl.BlockSpec(memory_space=pltpu.SMEM)
    patch = pltpu.VMEM((8, 2, PR, PC, CH), BF)
    padded = pltpu.VMEM((PR + 2, PC + 2, NF, CH), BF)
    clip_shape = x.shape[1:]
    dma = pltpu.SemaphoreType.DMA
    outs = jax.ShapeDtypeStruct(x.shape, BF)
    return pl.pallas_call(
        kernel,
        out_shape=(outs, outs),
        in_specs=[hbm, hbm, smem, hbm, hbm, hbm, smem, hbm, hbm, hbm, smem],
        out_specs=(hbm, hbm),
        scratch_shapes=[
            patch, patch, padded, padded, padded, padded,
            pltpu.VMEM((1024, CH), F32),
            pltpu.VMEM((1024, CH), F32),
            pltpu.VMEM((8, NF, CH), F32),
            pltpu.VMEM((NF, PR, PC, CH), BF),
            pltpu.VMEM(clip_shape, BF),
            pltpu.VMEM(clip_shape, BF),
            pltpu.VMEM(clip_shape, BF),
            pltpu.VMEM((3, 3, CH, CH), BF),
            pltpu.VMEM((3, 3, CH, CH), BF),
            pltpu.VMEM((3, 3, CH, CH), BF),
            pltpu.VMEM((CH, 3 * CH), BF),
            pltpu.VMEM((CH, CH), BF),
            pltpu.VMEM((CH, 4 * CH), BF),
            pltpu.VMEM((4 * CH, CH), BF),
            pltpu.VMEM((3, 3, CH, CH), BF),
            dma((11,)), dma((8,)), dma((8,)), dma((8,)), dma((8,)), dma((8,)), dma((8,)),
            dma((4, 8)), dma((4, 8)), dma((8,)), dma((8,)), dma((2,)),
        ],
        compiler_params=pltpu.CompilerParams(
            collective_id=0, has_side_effects=True, vmem_limit_bytes=40 * 1024 * 1024
        ),
        cost_estimate=pl.CostEstimate(flops=1_700_000_000, bytes_accessed=3_000_000, transcendentals=1_500_000),
        name="denoise",
    )(x, clip, picks, w_in, w_mid, proj, factors, w_up, w_dn, w_out, coefs)


def solution(mesh):
    clip = P("segment", "frame", "tile", None, None)
    kernel_spec = P("segment", None, None, None, None)
    in_specs = (
        clip, clip, P("segment", "frame"), kernel_spec, kernel_spec, P("segment", None, None, None),
        P("segment", None), P("segment", None, None), P("segment", None, None), kernel_spec, P("segment", None),
    )
    return jax.shard_map(local, mesh=mesh, in_specs=in_specs, out_specs=(clip, clip), check_vma=False)
```

time: 196 us -> 70.3 us (0.36)
  the two profiles are of different devices: /device:TPU:233 before, /device:TPU:17 now
where the time goes in v1:
time: 70.3 us; the launch traced here: 69.9 us
  Pallas kernels  58.3 us (83%)
  local copies, waits for them, and re-layouts  11 us (16%)
    pallas_call x1, Pallas kernels, local(): pl.pallas_call(kernel, out_shape=(outs, outs), in_specs=[hbm, hbm, smem,...  58.3 us
    unnamed x24, local copies, waits for them, and re-layouts  11 us

profile of v1, /device:TPU:17, one launch (start us, length us, event | category | flops | bytes accessed | tf_op | source)
XLA Modules:
  0.0 69.9 jit_solution(14366856387967212593)
XLA Ops:
  0.6 0.0 copy-start
  0.6 1.1 %copy-done = bf16[1,3,3,256,128]{4,3,2,1,0:T(8,128)(2,1)S(1)} copy-done((bf16[1,3,3,256,128]{4,3,2,1,0:T(8,128)(2,1)S(1)}, bf16[1,3,3,256,128]{4,3,2,1,0:T(8,128)(2,1)}, u32[]{:S(2)}) %copy-start) | copy-done | bytes 589848
  1.7 0.0 copy-start.1
  1.7 1.0 %copy-done.1 = bf16[1,3,3,128,128]{4,3,2,1,0:T(8,128)(2,1)S(1)} copy-done((bf16[1,3,3,128,128]{4,3,2,1,0:T(8,128)(2,1)S(1)}, bf16[1,3,3,128,128]{4,3,2,1,0:T(8,128)(2,1)}, u32[]{:S(2)}) %copy-start.1) | copy-done | bytes 294936
  2.7 0.0 copy-start.2
  2.7 1.0 %copy-done.2 = bf16[1,3,3,128,128]{4,3,2,1,0:T(8,128)(2,1)S(1)} copy-done((bf16[1,3,3,128,128]{4,3,2,1,0:T(8,128)(2,1)S(1)}, bf16[1,3,3,128,128]{4,3,2,1,0:T(8,128)(2,1)}, u32[]{:S(2)}) %copy-start.2) | copy-done | bytes 294936
  3.6 0.0 copy-start.3
  3.6 0.9 %copy-done.3 = bf16[1,2,8,64,128]{4,3,2,1,0:T(8,128)(2,1)S(1)} copy-done((bf16[1,2,8,64,128]{4,3,2,1,0:T(8,128)(2,1)S(1)}, bf16[1,2,8,64,128]{4,3,2,1,0:T(8,128)(2,1)}, u32[]{:S(2)}) %copy-start.3) | copy-done | bytes 262168
  4.6 0.0 copy-start.4
  4.6 0.9 %copy-done.4 = bf16[1,2,8,64,128]{4,3,2,1,0:T(8,128)(2,1)S(1)} copy-done((bf16[1,2,8,64,128]{4,3,2,1,0:T(8,128)(2,1)S(1)}, bf16[1,2,8,64,128]{4,3,2,1,0:T(8,128)(2,1)}, u32[]{:S(2)}) %copy-start.4) | copy-done | bytes 262168
  5.5 0.0 copy-start.5
  5.5 0.9 %copy-done.5 = bf16[1,4,128,128]{3,2,1,0:T(8,128)(2,1)S(1)} copy-done((bf16[1,4,128,128]{3,2,1,0:T(8,128)(2,1)S(1)}, bf16[1,4,128,128]{3,2,1,0:T(8,128)(2,1)}, u32[]{:S(2)}) %copy-start.5) | copy-done | bytes 131096
  6.4 0.0 copy-start.6
  6.4 0.9 %copy-done.6 = bf16[1,128,512]{2,1,0:T(8,128)(2,1)S(1)} copy-done((bf16[1,128,512]{2,1,0:T(8,128)(2,1)S(1)}, bf16[1,128,512]{2,1,0:T(8,128)(2,1)}, u32[]{:S(2)}) %copy-start.6) | copy-done | bytes 131096
  7.3 0.0 copy-start.7
  7.3 0.9 %copy-done.7 = bf16[1,512,128]{2,1,0:T(8,128)(2,1)S(1)} copy-done((bf16[1,512,128]{2,1,0:T(8,128)(2,1)S(1)}, bf16[1,512,128]{2,1,0:T(8,128)(2,1)}, u32[]{:S(2)}) %copy-start.7) | copy-done | bytes 131096
  8.2 0.0 copy-start.8
  8.2 0.7 copy-done.8
  8.9 0.0 copy-start.9
  8.9 0.7 copy-done.9
  9.6 0.7 copy-done.10
  10.2 58.3 %denoise.1 = (bf16[1,2,8,64,128]{4,3,2,1,0:T(8,128)(2,1)S(1)}, bf16[1,2,8,64,128]{4,3,2,1,0:T(8,128)(2,1)S(1)}) custom-call(bf16[1,2,8,64,128]{4,3,2,1,0:T(8,128)(2,1)S(1)} %copy-done.3, bf16[1,2,8,64,128]{4,3,2,1,0:T(8,128)(2,1)S(1)} %copy-done.4, s32[1,2]{1,0:T(1,128)S(1)} %copy-done.8, bf16[1,3,3,256,128]{4,3,2,1,0:T(8,128)(2,1)S(1)} %copy-done, ...), custom_call_target="tpu_custom_call" | custom-call | flops 1700000000 | bytes 3000000 | tf_op jit(solution)/shard_map/denoise/pallas_call | solution.py:323
  68.5 0.7 %copy.15 = bf16[1,2,8,64,128]{4,3,2,1,0:T(8,128)(2,1)} copy(bf16[1,2,8,64,128]{4,3,2,1,0:T(8,128)(2,1)S(1)} %get-tuple-element.4) | data formatting | bytes 524288
  69.2 0.7 %copy.16 = bf16[1,2,8,64,128]{4,3,2,1,0:T(8,128)(2,1)} copy(bf16[1,2,8,64,128]{4,3,2,1,0:T(8,128)(2,1)S(1)} %get-tuple-element.5) | data formatting | bytes 524288
  (1 shorter events, 0.0 us)
Async XLA Ops:
  0.6 1.1 %copy-start = (bf16[1,3,3,256,128]{4,3,2,1,0:T(8,128)(2,1)S(1)}, bf16[1,3,3,256,128]{4,3,2,1,0:T(8,128)(2,1)}, u32[]{:S(2)}) copy-start(bf16[1,3,3,256,128]{4,3,2,1,0:T(8,128)(2,1)} %w_in.1) | copy-start | bytes 1769476
  1.7 1.0 %copy-start.1 = (bf16[1,3,3,128,128]{4,3,2,1,0:T(8,128)(2,1)S(1)}, bf16[1,3,3,128,128]{4,3,2,1,0:T(8,128)(2,1)}, u32[]{:S(2)}) copy-start(bf16[1,3,3,128,128]{4,3,2,1,0:T(8,128)(2,1)} %w_mid.1) | copy-start | bytes 884740
  2.7 1.0 %copy-start.2 = (bf16[1,3,3,128,128]{4,3,2,1,0:T(8,128)(2,1)S(1)}, bf16[1,3,3,128,128]{4,3,2,1,0:T(8,128)(2,1)}, u32[]{:S(2)}) copy-start(bf16[1,3,3,128,128]{4,3,2,1,0:T(8,128)(2,1)} %w_out.1) | copy-start | bytes 884740
  3.6 0.9 %copy-start.3 = (bf16[1,2,8,64,128]{4,3,2,1,0:T(8,128)(2,1)S(1)}, bf16[1,2,8,64,128]{4,3,2,1,0:T(8,128)(2,1)}, u32[]{:S(2)}) copy-start(bf16[1,2,8,64,128]{4,3,2,1,0:T(8,128)(2,1)} %x_hbm.1) | copy-start | bytes 786436
  4.6 0.9 %copy-start.4 = (bf16[1,2,8,64,128]{4,3,2,1,0:T(8,128)(2,1)S(1)}, bf16[1,2,8,64,128]{4,3,2,1,0:T(8,128)(2,1)}, u32[]{:S(2)}) copy-start(bf16[1,2,8,64,128]{4,3,2,1,0:T(8,128)(2,1)} %clip_hbm.1) | copy-start | bytes 786436
  5.5 0.9 %copy-start.5 = (bf16[1,4,128,128]{3,2,1,0:T(8,128)(2,1)S(1)}, bf16[1,4,128,128]{3,2,1,0:T(8,128)(2,1)}, u32[]{:S(2)}) copy-start(bf16[1,4,128,128]{3,2,1,0:T(8,128)(2,1)} %proj.1) | copy-start | bytes 393220
  6.4 0.9 %copy-start.6 = (bf16[1,128,512]{2,1,0:T(8,128)(2,1)S(1)}, bf16[1,128,512]{2,1,0:T(8,128)(2,1)}, u32[]{:S(2)}) copy-start(bf16[1,128,512]{2,1,0:T(8,128)(2,1)} %w_up.1) | copy-start | bytes 393220
  7.3 0.9 %copy-start.7 = (bf16[1,512,128]{2,1,0:T(8,128)(2,1)S(1)}, bf16[1,512,128]{2,1,0:T(8,128)(2,1)}, u32[]{:S(2)}) copy-start(bf16[1,512,128]{2,1,0:T(8,128)(2,1)} %w_dn.1) | copy-start | bytes 393220
  8.2 0.7 copy-start.8
  8.9 0.7 copy-start.9
  9.6 0.7 copy-start.10

commit v2 on v1

v2 whole, which is shorter than its diff:
```python
import functools

import jax
import jax.numpy as jnp
from jax import lax
from jax.experimental import pallas as pl
from jax.experimental.pallas import tpu as pltpu
from jax.sharding import PartitionSpec as P

MESH = pl.DeviceIdType.MESH
BF = jnp.bfloat16
F32 = jnp.float32
PR, PC, NF, CH = 4, 16, 16, 128
DIRS = [(-1, 0), (1, 0), (0, -1), (0, 1), (-1, -1), (-1, 1), (1, -1), (1, 1)]
ROWS, COLS, CORNERS = (0, 1), (2, 3), (4, 5, 6, 7)


def dot(a, b):
    return jnp.dot(a, b, preferred_element_type=F32)


def lane_sums(v, ones):
    hi = v.astype(BF)
    lo = (v - hi.astype(F32)).astype(BF)
    return dot(jnp.concatenate([hi, lo], axis=1), jnp.concatenate([ones, ones], axis=0))


def silu(v):
    half = 0.5 * v
    return half + half * jnp.tanh(half)


def kernel(
    x_hbm, clip_hbm, picks_hbm, w_in, w_mid, proj, factors_hbm, w_up, w_dn, w_out,
    eps_out,
    picks, factors, raw_n, raw_c, xn, xc, hb, cb, top, bot, lef, rig, acc, res, pk, send_e,
    v_in_n, v_in_c, v_mid, v_qkv, v_o, v_up, v_dn, v_out,
    s_w, s_pk, r_pk, s_c, r_c, s_n, r_n, s_h, r_h, s_e, r_e,
):
    s = lax.axis_index("segment")
    t = lax.axis_index("tile")
    d = lax.axis_index("frame")
    i, j = lax.rem(d, 2), lax.div(d, 2)
    big_row = 2 * t + i
    last_row = 2 * lax.axis_size("tile") - 1
    last_segment = lax.axis_size("segment") - 1

    def exists(dr, dc):
        row, col = big_row + dr, j + dc
        return (row >= 0) & (row <= last_row) & (col >= 0) & (col <= 3)

    def neighbour(dr, dc):
        row, col = big_row + dr, j + dc
        return {"tile": lax.div(row, 2), "frame": 2 * col + lax.rem(row, 2)}

    def in_group(k):
        return lax.rem(d + k, 8)

    def signal(device):
        pl.semaphore_signal(barrier, inc=1, device_id=device, device_id_type=MESH)

    for ref in (top, bot, lef, rig):
        ref[...] = jnp.zeros(ref.shape, BF)

    barrier = pltpu.get_barrier_semaphore()

    @pl.when(s > 0)
    def _():
        for k in range(8):
            signal({"segment": s - 1, "frame": in_group(k)})

    for k in range(1, 8):
        signal({"frame": in_group(k)})
    over = 2 * i - 1
    for dc in (-1, 0, 1):

        @pl.when(exists(over, dc))
        def _(dc=dc):
            signal(neighbour(over, dc))

    weights = [
        (picks_hbm, picks),
        (w_in.at[0, :, :, 0:CH, :], v_in_n),
        (w_in.at[0, :, :, CH : 2 * CH, :], v_in_c),
        (factors_hbm, factors),
        (w_mid.at[0], v_mid),
        (proj.at[0, 0], v_qkv.at[:, 0:CH]),
        (proj.at[0, 1], v_qkv.at[:, CH : 2 * CH]),
        (proj.at[0, 2], v_qkv.at[:, 2 * CH : 3 * CH]),
        (proj.at[0, 3], v_o),
        (w_up.at[0], v_up),
        (w_dn.at[0], v_dn),
        (w_out.at[0], v_out),
    ]
    loads = [pltpu.make_async_copy(a, b, s_w.at[q]) for q, (a, b) in enumerate(weights)]
    for load in loads:
        load.start()
    for buf in (xn, xc, hb, cb):
        buf[0] = jnp.zeros((PC + 2, NF, CH), BF)
        buf[PR + 1] = jnp.zeros((PC + 2, NF, CH), BF)
        buf[:, 0:1] = jnp.zeros((PR + 2, 1, NF, CH), BF)
        buf[:, PC + 1 : PC + 2] = jnp.zeros((PR + 2, 1, NF, CH), BF)
    partners = 7 + jnp.where(s < last_segment, 8, 0)
    for dc in (-1, 0, 1):
        partners = partners + jnp.where(exists(over, dc), 1, 0)
    pl.semaphore_wait(barrier, partners)

    def patch_of(ref, c):
        return ref.at[0, :, pl.ds(PR * lax.rem(c, 2), PR), pl.ds(pl.multiple_of(PC * lax.div(c, 2), PC), PC), :]

    def clip_copy(k):
        return pltpu.make_async_remote_copy(
            src_ref=patch_of(clip_hbm, in_group(k)),
            dst_ref=raw_c.at[d],
            send_sem=s_c.at[k],
            recv_sem=r_c.at[k],
            device_id={"segment": s + 1, "frame": in_group(k)},
            device_id_type=MESH,
        )

    @pl.when(s < last_segment)
    def _():
        for k in range(8):
            clip_copy(k).start()

    pick_copies, noisy_copies = [], []
    own_noisy = pltpu.make_async_copy(patch_of(x_hbm, d), raw_n.at[d], s_n.at[0])
    own_noisy.start()
    for k in range(1, 8):
        noisy_copies.append(
            pltpu.make_async_remote_copy(
                src_ref=patch_of(x_hbm, in_group(k)),
                dst_ref=raw_n.at[d],
                send_sem=s_n.at[k],
                recv_sem=r_n.at[k],
                device_id={"frame": in_group(k)},
                device_id_type=MESH,
            )
        )
        noisy_copies[-1].start()
    loads[0].wait()
    frame_row = lax.broadcasted_iota(jnp.int32, (NF, CH), 0)
    pk[d] = jnp.where(frame_row == 2 * d, picks[0, 0], jnp.where(frame_row == 2 * d + 1, picks[0, 1], 0)).astype(F32)
    for k in range(1, 8):
        pick_copies.append(
            pltpu.make_async_remote_copy(
                src_ref=pk.at[d],
                dst_ref=pk.at[d],
                send_sem=s_pk.at[k],
                recv_sem=r_pk.at[k],
                device_id={"frame": in_group(k)},
                device_id_type=MESH,
            )
        )
        pick_copies[-1].start()

    r_i = lax.broadcasted_iota(jnp.int32, (256, 256), 0)
    c_i = lax.broadcasted_iota(jnp.int32, (256, 256), 1)
    r_hi, r_lo, c_hi, c_lo = r_i // 16, r_i % 16, c_i // 16, c_i % 16
    swap = jnp.where((r_hi == c_lo) & (r_lo == c_hi), 1.0, 0.0).astype(BF)

    def halo_copy(buf, n, k):
        inner = slice(1, PC + 1)
        rows = slice(1, PR + 1)
        ends = [
            (buf.at[1, inner], bot.at[n, inner]),
            (buf.at[PR, inner], top.at[n, inner]),
            (buf.at[rows, 1], rig.at[n, rows]),
            (buf.at[rows, PC], lef.at[n, rows]),
            (buf.at[1, 1], bot.at[n, PC + 1]),
            (buf.at[1, PC], bot.at[n, 0]),
            (buf.at[PR, 1], top.at[n, PC + 1]),
            (buf.at[PR, PC], top.at[n, 0]),
        ]
        src, dst = ends[k]
        return pltpu.make_async_remote_copy(
            src_ref=src,
            dst_ref=dst,
            send_sem=s_h.at[n, k],
            recv_sem=r_h.at[n, k],
            device_id=neighbour(*DIRS[k]),
            device_id_type=MESH,
        )

    def halo_start(buf, n):
        for k in range(8):
            pl.when(exists(*DIRS[k]))(halo_copy(buf, n, k).start)

    def halo_wait(buf, n, which):
        for k in which:
            dr, dc = DIRS[k]
            pl.when(exists(-dr, -dc))(halo_copy(buf, n, k).wait_recv)

    def halo_sent(buf, n):
        for k in range(8):
            pl.when(exists(*DIRS[k]))(halo_copy(buf, n, k).wait_send)

    def conv(buf, w, row, rows):
        n = rows * PC * NF
        parts = [
            buf[row + dr : row + dr + rows, dc : dc + PC].reshape(n, CH) for dr in range(3) for dc in range(3)
        ]
        return dot(jnp.concatenate(parts, axis=1), w[...].reshape(9 * CH, CH)).reshape(rows, PC, NF, CH)

    def add_rows(to, n, w):
        for row, ref, tap in ((0, top, 0), (PR - 1, bot, 2)):
            parts = [ref[n, dc : dc + PC].reshape(PC * NF, CH) for dc in range(3)]
            to[row] += dot(jnp.concatenate(parts, axis=1), w[tap].reshape(3 * CH, CH)).reshape(PC, NF, CH)

    def add_cols(to, n, w):
        for col, ref, tap in ((0, lef, 0), (PC - 1, rig, 2)):
            parts = [ref[n, dr : dr + PR].reshape(PR * NF, CH) for dr in range(3)]
            to[:, col] += dot(jnp.concatenate(parts, axis=1), w[:, tap].reshape(3 * CH, CH)).reshape(PR, NF, CH)

    own_noisy.wait()
    for copy in noisy_copies:
        copy.wait_recv()
    for row in range(PR):
        xn[row + 1, 1 : PC + 1] = dot(swap, raw_n[:, :, row].reshape(256, CH)).astype(BF).reshape(PC, NF, CH)
    halo_start(xn, 0)
    loads[1].wait()
    for row in (0, 2):
        acc[row : row + 2] = conv(xn, v_in_n, row, 2)

    for copy in pick_copies:
        copy.wait_recv()
    pick_rows = pk[0]
    for q in range(1, 8):
        pick_rows = pick_rows + pk[q]
    pick_rows = jnp.broadcast_to(pick_rows[None], (16, NF, CH)).reshape(256, CH)
    pick_rows = jnp.concatenate([pick_rows, pick_rows], axis=1)
    choose = jnp.where((r_hi == c_lo) & (pick_rows == c_hi.astype(F32)), 1.0, 0.0).astype(BF)

    @pl.when(s == 0)
    def _():
        raw_c[...] = jnp.zeros(raw_c.shape, BF)

    @pl.when(s > 0)
    def _():
        for k in range(8):
            clip_copy(k).wait_recv()

    for row in range(PR):
        xc[row + 1, 1 : PC + 1] = dot(choose, raw_c[:, :, row].reshape(256, CH)).astype(BF).reshape(PC, NF, CH)
    halo_start(xc, 1)
    for load in loads[2:]:
        load.wait()
    for row in (0, 2):
        acc[row : row + 2] += conv(xc, v_in_c, row, 2)
    halo_wait(xn, 0, range(8))
    add_rows(acc, 0, v_in_n)
    add_cols(acc, 0, v_in_n)
    halo_wait(xc, 1, range(8))
    add_rows(acc, 1, v_in_c)
    add_cols(acc, 1, v_in_c)
    hb[1 : PR + 1, 1 : PC + 1] = silu(acc[...]).astype(BF)
    halo_start(hb, 2)

    lane_r = lax.broadcasted_iota(jnp.int32, (CH, CH), 0)
    lane_c = lax.broadcasted_iota(jnp.int32, (CH, CH), 1)
    ones = jnp.full((CH, CH), 1.0, BF)
    by_head = jnp.where(lane_r // 64 == lane_c // 64, 1.0, 0.0).astype(BF)
    first_head = lane_c < 64
    other_pixel = jnp.where(lane_r // 16 == lane_c // 16, 0.0, -1e30)
    for row in (0, 2):
        skip = hb[row + 1 : row + 3, 1 : PC + 1].astype(F32)
        res[row : row + 2] = skip + conv(hb, v_mid, row, 2)
    halo_sent(xn, 0)
    halo_sent(xc, 1)

    def two_rows(rows):
        a = jnp.concatenate([res[row].reshape(256, CH) for row in rows], axis=0)
        u = (a * lax.rsqrt(lane_sums(a * a, ones) * (1 / 128) + 1e-6)).astype(BF)
        qkv = dot(u, v_qkv[...])
        q, k, v = qkv[:, 0:CH], qkv[:, CH : 2 * CH], qkv[:, 2 * CH : 3 * CH].astype(BF)
        qn = (q * lax.rsqrt(lane_sums(q * q, by_head) * (1 / 64) + 1e-6)).astype(BF)
        kn = (k * lax.rsqrt(lane_sums(k * k, by_head) * (1 / 64) + 1e-6)).astype(BF)
        parts = []
        zero = jnp.zeros((CH, CH), BF)
        for g in range(4):
            qg, kg, vg = (z[g * CH : (g + 1) * CH] for z in (qn, kn, v))
            both = jnp.concatenate([jnp.where(first_head, qg, zero), jnp.where(first_head, zero, qg)], axis=0)
            sc = lax.dot_general(both, kg, (((1,), (1,)), ((), ())), preferred_element_type=F32)
            sc = jnp.concatenate(
                [sc[h * CH : (h + 1) * CH] * (factors[0, h] * (1 / 64)) + other_pixel for h in range(2)], axis=0
            )
            e = jnp.exp(sc - jnp.max(sc, axis=1, keepdims=True))
            total = jnp.sum(e, axis=1, keepdims=True)
            o = dot(e.astype(BF), vg) / total
            parts.append(jnp.where(first_head, o[:CH], o[CH:]).astype(BF))
        b = a + dot(jnp.concatenate(parts, axis=0), v_o[...])
        r = (b * lax.rsqrt(lane_sums(b * b, ones) * (1 / 128) + 1e-6)).astype(BF)
        m = silu(dot(r, v_up[...])).astype(BF)
        c = (b + dot(m, v_dn[...])).astype(BF)
        for q, row in enumerate(rows):
            cb[row + 1, 1 : PC + 1] = c[q * 256 : (q + 1) * 256].reshape(PC, NF, CH)

    halo_wait(hb, 2, COLS)
    add_cols(res, 2, v_mid)
    two_rows((1, 2))
    halo_wait(hb, 2, ROWS + CORNERS)
    add_rows(res, 2, v_mid)
    two_rows((0, 3))
    halo_start(cb, 3)
    halo_sent(hb, 2)
    for row in (0, 2):
        acc[row : row + 2] = conv(cb, v_out, row, 2)
    halo_wait(cb, 3, COLS)
    add_cols(acc, 3, v_out)

    def eps_copy(k, n, rows):
        size = rows.stop - rows.start
        src = send_e.at[pl.ds(2 * in_group(k), 2), rows]
        dst = eps_out.at[0, :, pl.ds(PR * i + rows.start, size), pl.ds(pl.multiple_of(PC * j, PC), PC), :]
        if k == 0:
            return pltpu.make_async_copy(src, dst, s_e.at[n, 0])
        return pltpu.make_async_remote_copy(
            src_ref=src,
            dst_ref=dst,
            send_sem=s_e.at[n, k],
            recv_sem=r_e.at[n, k],
            device_id={"frame": in_group(k)},
            device_id_type=MESH,
        )

    eps_copies = []

    def give_back(n, rows):
        for row in range(rows.start, rows.stop):
            part = dot(swap, acc[row].reshape(256, CH).astype(BF)).astype(BF)
            send_e[:, row] = part.reshape(NF, PC, CH)
        for k in (*range(1, 8), 0):
            eps_copies.append((k, eps_copy(k, n, rows)))
            eps_copies[-1][1].start()

    give_back(0, slice(1, 3))
    halo_wait(cb, 3, ROWS + CORNERS)
    add_rows(acc, 3, v_out)
    give_back(1, slice(0, 1))
    give_back(2, slice(3, 4))
    for copy in pick_copies + noisy_copies:
        copy.wait_send()

    @pl.when(s < last_segment)
    def _():
        for k in range(8):
            clip_copy(k).wait_send()

    halo_sent(cb, 3)
    for k, copy in eps_copies:
        copy.wait()


def local(x, clip, picks, w_in, w_mid, proj, factors, w_up, w_dn, w_out, coefs):
    hbm = pl.BlockSpec(memory_space=pltpu.HBM)
    patch = pltpu.VMEM((8, 2, PR, PC, CH), BF)
    padded = pltpu.VMEM((PR + 2, PC + 2, NF, CH), BF)
    side = pltpu.VMEM((4, PC + 2, NF, CH), BF)
    upright = pltpu.VMEM((4, PR + 2, NF, CH), BF)
    sums = pltpu.VMEM((PR, PC, NF, CH), F32)
    taps = pltpu.VMEM((3, 3, CH, CH), BF)
    dma = pltpu.SemaphoreType.DMA
    eps = pl.pallas_call(
        kernel,
        out_shape=jax.ShapeDtypeStruct(x.shape, BF),
        in_specs=[hbm] * 10,
        out_specs=hbm,
        scratch_shapes=[
            pltpu.SMEM((1, 2), jnp.int32),
            pltpu.SMEM((1, 2), F32),
            patch, patch, padded, padded, padded, padded, side, side, upright, upright, sums, sums,
            pltpu.VMEM((8, NF, CH), F32),
            pltpu.VMEM((NF, PR, PC, CH), BF),
            taps, taps, taps,
            pltpu.VMEM((CH, 3 * CH), BF),
            pltpu.VMEM((CH, CH), BF),
            pltpu.VMEM((CH, 4 * CH), BF),
            pltpu.VMEM((4 * CH, CH), BF),
            taps,
            dma((12,)), dma((8,)), dma((8,)), dma((8,)), dma((8,)), dma((8,)), dma((8,)),
            dma((4, 8)), dma((4, 8)), dma((3, 8)), dma((3, 8)),
        ],
        compiler_params=pltpu.CompilerParams(
            collective_id=0, has_side_effects=True, vmem_limit_bytes=60 * 1024 * 1024
        ),
        cost_estimate=pl.CostEstimate(flops=1_700_000_000, bytes_accessed=3_000_000, transcendentals=1_500_000),
        name="denoise",
    )(x, clip, picks, w_in, w_mid, proj, factors, w_up, w_dn, w_out)
    denoised = coefs[0, 0] * x.astype(F32) - coefs[0, 1] * eps.astype(F32)
    return denoised.astype(BF), eps


def solution(mesh):
    clip = P("segment", "frame", "tile", None, None)
    kernel_spec = P("segment", None, None, None, None)
    in_specs = (
        clip, clip, P("segment", "frame"), kernel_spec, kernel_spec, P("segment", None, None, None),
        P("segment", None), P("segment", None, None), P("segment", None, None), kernel_spec, P("segment", None),
    )
    return jax.shard_map(local, mesh=mesh, in_specs=in_specs, out_specs=(clip, clip), check_vma=False)
```

time: 70.3 us -> 51.5 us (0.73)
  the two profiles are of different devices: /device:TPU:17 before, /device:TPU:233 now
where the time goes in v2:
time: 51.5 us; the launch traced here: 51.2 us
  Pallas kernels  45.4 us (88%)
  other arithmetic  3.13 us (6%)
  local copies, waits for them, and re-layouts  2.1 us (4%)
  between operations  0.66 us (1%)
    pallas_call x1, Pallas kernels, local(): pl.pallas_call(kernel, out_shape=jax.ShapeDtypeStruct(x.shape, BF), in_sp...  45.4 us
    convert_element_type x1, other arithmetic, local(): return (denoised.astype(BF), eps)  3.13 us
    slice x1, local copies, waits for them, and re-layouts, local(): denoised = coefs[0, 0] * x.astype(F32) - coefs[0, 1] * eps.astype(F32)  1.39 us

profile of v2, /device:TPU:233, one launch (start us, length us, event | category | flops | bytes accessed | tf_op | source)
XLA Modules:
  0.0 51.2 jit_solution(13826691805511702270)
XLA Ops:
  0.6 1.4 %fusion = (f32[1,1]{1,0:T(1,128)}, f32[1,1]{1,0:T(1,128)}) fusion(f32[1,2]{1,0:T(1,128)} %param.21), kind=kLoop, calls=%fused_computation.1 | loop fusion | bytes 16 | tf_op jit(solution)/shard_map/slice | solution.py:389
  2.0 0.0 copy-start.1
  2.0 45.4 %denoise.1 = bf16[1,2,8,64,128]{4,3,2,1,0:T(8,128)(2,1)} custom-call(bf16[1,2,8,64,128]{4,3,2,1,0:T(8,128)(2,1)} %x_hbm.1, bf16[1,2,8,64,128]{4,3,2,1,0:T(8,128)(2,1)} %clip_hbm.1, s32[1,2]{1,0:T(1,128)} %picks_hbm.1, bf16[1,3,3,256,128]{4,3,2,1,0:T(8,128)(2,1)} %w_in.1, bf16[1,3,3,128,128]{4,3,2,1,0:T(8,128)(2,1)} %w_mid.1, bf16[1,4,128,128]{3,2,1,0:T(8,128)(2,1)} %proj.1, ...), custom_call_target="tpu_custom_call" | custom-call | flops 1700000000 | bytes 3000000 | tf_op jit(solution)/shard_map/denoise/pallas_call | solution.py:363
  47.4 0.0 copy-done.1
  47.4 0.0 copy-start
  47.4 3.1 %subtract_convert_fusion = bf16[1,2,8,64,128]{4,3,2,1,0:T(8,128)(2,1)} fusion(bf16[1,2,8,64,128]{4,3,2,1,0:T(8,128)(2,1)} %denoise.1, bf16[1,2,8,64,128]{4,3,2,1,0:T(8,128)(2,1)S(1)} %copy-done.1, f32[]{:T(128)} %bitcast.1, f32[]{:T(128)} %bitcast), kind=kLoop, calls=%fused_computation | loop fusion | flops 786432 | bytes 786440 | tf_op jit(solution)/shard_map/convert_element_type | solution.py:390
  50.5 0.0 copy-done
  50.5 0.7 %copy.14 = bf16[1,2,8,64,128]{4,3,2,1,0:T(8,128)(2,1)} copy(bf16[1,2,8,64,128]{4,3,2,1,0:T(8,128)(2,1)S(1)} %copy-done) | data formatting | bytes 524288
Async XLA Ops:
  2.0 45.4 %copy-start.1 = (bf16[1,2,8,64,128]{4,3,2,1,0:T(8,128)(2,1)S(1)}, bf16[1,2,8,64,128]{4,3,2,1,0:T(8,128)(2,1)}, u32[]{:S(2)}) copy-start(bf16[1,2,8,64,128]{4,3,2,1,0:T(8,128)(2,1)} %x_hbm.1) | copy-start | bytes 786436
  47.4 3.1 %copy-start = (bf16[1,2,8,64,128]{4,3,2,1,0:T(8,128)(2,1)S(1)}, bf16[1,2,8,64,128]{4,3,2,1,0:T(8,128)(2,1)}, u32[]{:S(2)}) copy-start(bf16[1,2,8,64,128]{4,3,2,1,0:T(8,128)(2,1)} %denoise.1) | copy-start | bytes 786436

commit v3 on v2

--- a/solution.py
+++ b/solution.py
@@ -11,6 +11,7 @@
 BF = jnp.bfloat16
 F32 = jnp.float32
 PR, PC, NF, CH = 4, 16, 16, 128
+TR, W = 8, 64
 DIRS = [(-1, 0), (1, 0), (0, -1), (0, 1), (-1, -1), (-1, 1), (1, -1), (1, 1)]
 ROWS, COLS, CORNERS = (0, 1), (2, 3), (4, 5, 6, 7)
 
@@ -31,18 +32,19 @@
 
 
 def kernel(
-    x_hbm, clip_hbm, picks_hbm, w_in, w_mid, proj, factors_hbm, w_up, w_dn, w_out,
-    eps_out,
-    picks, factors, raw_n, raw_c, xn, xc, hb, cb, top, bot, lef, rig, acc, res, pk, send_e,
+    x_hbm, clip_hbm, picks_hbm, w_in, w_mid, proj, factors_hbm, w_up, w_dn, w_out, coefs_hbm,
+    den_out, eps_out,
+    picks, factors, coefs, raw_n, raw_c, xn, xc, hb, top, bot, lef, rig, acc, res, pk, send_c, frames_c, xv,
     v_in_n, v_in_c, v_mid, v_qkv, v_o, v_up, v_dn, v_out,
-    s_w, s_pk, r_pk, s_c, r_c, s_n, r_n, s_h, r_h, s_e, r_e,
+    s_w, s_pk, r_pk, s_c, r_c, s_n, r_n, s_h, r_h, s_e, r_e, s_o, r_o,
 ):
     s = lax.axis_index("segment")
     t = lax.axis_index("tile")
     d = lax.axis_index("frame")
     i, j = lax.rem(d, 2), lax.div(d, 2)
     big_row = 2 * t + i
-    last_row = 2 * lax.axis_size("tile") - 1
+    last_tile = lax.axis_size("tile") - 1
+    last_row = 2 * last_tile + 1
     last_segment = lax.axis_size("segment") - 1
 
     def exists(dr, dc):
@@ -61,6 +63,8 @@
 
     for ref in (top, bot, lef, rig):
         ref[...] = jnp.zeros(ref.shape, BF)
+    frames_c[:, 0:1] = jnp.zeros((2, 1, W, CH), BF)
+    frames_c[:, TR + 1 :] = jnp.zeros((2, 1, W, CH), BF)
 
     barrier = pltpu.get_barrier_semaphore()
 
@@ -71,12 +75,19 @@
 
     for k in range(1, 8):
         signal({"frame": in_group(k)})
-    over = 2 * i - 1
-    for dc in (-1, 0, 1):
-
-        @pl.when(exists(over, dc))
-        def _(dc=dc):
-            signal(neighbour(over, dc))
+
+    @pl.when(t > 0)
+    def _():
+        for q in range(4):
+            signal({"tile": t - 1, "frame": 2 * q + 1})
+
+    @pl.when(t < last_tile)
+    def _():
+        for q in range(4):
+            signal({"tile": t + 1, "frame": 2 * q})
+
+    over = t + 2 * i - 1
+    over_exists = (over >= 0) & (over <= last_tile)
 
     weights = [
         (picks_hbm, picks),
@@ -90,20 +101,19 @@
         (proj.at[0, 3], v_o),
         (w_up.at[0], v_up),
         (w_dn.at[0], v_dn),
-        (w_out.at[0], v_out),
+        *((w_out.at[0, :, q], v_out.at[:, :, q * CH : (q + 1) * CH]) for q in range(3)),
+        (coefs_hbm, coefs),
+        (x_hbm.at[0], xv),
     ]
     loads = [pltpu.make_async_copy(a, b, s_w.at[q]) for q, (a, b) in enumerate(weights)]
     for load in loads:
         load.start()
-    for buf in (xn, xc, hb, cb):
+    for buf in (xn, xc, hb):
         buf[0] = jnp.zeros((PC + 2, NF, CH), BF)
         buf[PR + 1] = jnp.zeros((PC + 2, NF, CH), BF)
         buf[:, 0:1] = jnp.zeros((PR + 2, 1, NF, CH), BF)
         buf[:, PC + 1 : PC + 2] = jnp.zeros((PR + 2, 1, NF, CH), BF)
-    partners = 7 + jnp.where(s < last_segment, 8, 0)
-    for dc in (-1, 0, 1):
-        partners = partners + jnp.where(exists(over, dc), 1, 0)
-    pl.semaphore_wait(barrier, partners)
+    pl.semaphore_wait(barrier, 7 + jnp.where(s < last_segment, 8, 0) + jnp.where(over_exists, 8, 0))
 
     def patch_of(ref, c):
         return ref.at[0, :, pl.ds(PR * lax.rem(c, 2), PR), pl.ds(pl.multiple_of(PC * lax.div(c, 2), PC), PC), :]
@@ -183,7 +193,7 @@
         )
 
     def halo_start(buf, n):
-        for k in range(8):
+        for k in COLS + CORNERS + ROWS:
             pl.when(exists(*DIRS[k]))(halo_copy(buf, n, k).start)
 
     def halo_wait(buf, n, which):
@@ -293,51 +303,66 @@
         m = silu(dot(r, v_up[...])).astype(BF)
         c = (b + dot(m, v_dn[...])).astype(BF)
         for q, row in enumerate(rows):
-            cb[row + 1, 1 : PC + 1] = c[q * 256 : (q + 1) * 256].reshape(PC, NF, CH)
-
-    halo_wait(hb, 2, COLS)
-    add_cols(res, 2, v_mid)
-    two_rows((1, 2))
-    halo_wait(hb, 2, ROWS + CORNERS)
-    add_rows(res, 2, v_mid)
-    two_rows((0, 3))
-    halo_start(cb, 3)
-    halo_sent(hb, 2)
-    for row in (0, 2):
-        acc[row : row + 2] = conv(cb, v_out, row, 2)
-    halo_wait(cb, 3, COLS)
-    add_cols(acc, 3, v_out)
-
-    def eps_copy(k, n, rows):
-        size = rows.stop - rows.start
-        src = send_e.at[pl.ds(2 * in_group(k), 2), rows]
-        dst = eps_out.at[0, :, pl.ds(PR * i + rows.start, size), pl.ds(pl.multiple_of(PC * j, PC), PC), :]
-        if k == 0:
-            return pltpu.make_async_copy(src, dst, s_e.at[n, 0])
+            part = dot(swap, c[q * 256 : (q + 1) * 256]).astype(BF)
+            send_c[:, row] = part.reshape(NF, PC, CH)
+
+    def back_copy(n, k, first, size, to_row, device):
+        frame = device["frame"]
+        src = send_c.at[pl.ds(2 * frame, 2), first : first + size]
+        dst = frames_c.at[:, pl.ds(to_row, size), pl.ds(pl.multiple_of(PC * j, PC), PC), :]
         return pltpu.make_async_remote_copy(
             src_ref=src,
             dst_ref=dst,
             send_sem=s_e.at[n, k],
             recv_sem=r_e.at[n, k],
-            device_id={"frame": in_group(k)},
+            device_id=device,
             device_id_type=MESH,
         )
 
-    eps_copies = []
-
-    def give_back(n, rows):
-        for row in range(rows.start, rows.stop):
-            part = dot(swap, acc[row].reshape(256, CH).astype(BF)).astype(BF)
-            send_e[:, row] = part.reshape(NF, PC, CH)
-        for k in (*range(1, 8), 0):
-            eps_copies.append((k, eps_copy(k, n, rows)))
-            eps_copies[-1][1].start()
-
-    give_back(0, slice(1, 3))
-    halo_wait(cb, 3, ROWS + CORNERS)
-    add_rows(acc, 3, v_out)
-    give_back(1, slice(0, 1))
-    give_back(2, slice(3, 4))
+    def give_back(n, first, size):
+        copies = [back_copy(n, k, first, size, 1 + PR * i + first, {"frame": in_group(k)}) for k in range(1, 8)]
+        for copy in copies:
+            copy.start()
+        own = pltpu.make_async_copy(
+            send_c.at[pl.ds(2 * d, 2), first : first + size],
+            frames_c.at[:, pl.ds(1 + PR * i + first, size), pl.ds(pl.multiple_of(PC * j, PC), PC), :],
+            s_e.at[n, 0],
+        )
+        own.start()
+        return [*copies, own]
+
+    halo_wait(hb, 2, COLS)
+    add_cols(res, 2, v_mid)
+    two_rows((1, 2))
+    back = give_back(0, 1, 2)
+    halo_wait(hb, 2, ROWS + CORNERS)
+    add_rows(res, 2, v_mid)
+    two_rows((0, 3))
+
+    def over_copy(k, upper):
+        first, to_row = (0, TR + 1) if upper else (PR - 1, 0)
+        device = {"tile": over, "frame": in_group(k)}
+        src = send_c.at[pl.ds(2 * in_group(k), 2), first : first + 1]
+        dst = frames_c.at[:, to_row : to_row + 1, pl.ds(pl.multiple_of(PC * j, PC), PC), :]
+        return pltpu.make_async_remote_copy(
+            src_ref=src,
+            dst_ref=dst,
+            send_sem=s_o.at[k],
+            recv_sem=r_o.at[1 if upper else 0, j],
+            device_id=device,
+            device_id_type=MESH,
+        )
+
+    for upper in (True, False):
+
+        @pl.when(over_exists & (i == (0 if upper else 1)))
+        def _(upper=upper):
+            for k in range(8):
+                over_copy(k, upper).start()
+
+    back += give_back(1, 0, 1)
+    back += give_back(2, PR - 1, 1)
+    halo_sent(hb, 2)
     for copy in pick_copies + noisy_copies:
         copy.wait_send()
 
@@ -346,48 +371,102 @@
         for k in range(8):
             clip_copy(k).wait_send()
 
-    halo_sent(cb, 3)
-    for k, copy in eps_copies:
+    for copy in back:
         copy.wait()
 
+    def over_arrived(side, q, to_row):
+        at = frames_c.at[:, to_row : to_row + 1, q * PC : (q + 1) * PC, :]
+        pltpu.make_async_remote_copy(
+            src_ref=at, dst_ref=at, send_sem=s_o.at[0], recv_sem=r_o.at[side, q], device_id={"frame": d}, device_id_type=MESH
+        ).wait_recv()
+
+    @pl.when(t > 0)
+    def _():
+        for q in range(4):
+            over_arrived(0, q, 0)
+
+    @pl.when(t < last_tile)
+    def _():
+        for q in range(4):
+            over_arrived(1, q, TR + 1)
+
+    column = lax.rem(lax.broadcasted_iota(jnp.int32, (TR * W, CH), 0), W)
+    for f in range(2):
+        rows = [frames_c[f, dr : dr + TR].reshape(TR * W, CH) for dr in range(3)]
+        out = dot(jnp.concatenate(rows, axis=1), v_out[...].reshape(3 * CH, 3 * CH))
+        left = jnp.where(column == 0, 0.0, pltpu.roll(out[:, 0:CH], 1, 0))
+        right = jnp.where(column == W - 1, 0.0, pltpu.roll(out[:, 2 * CH :], TR * W - 1, 0))
+        eps = out[:, CH : 2 * CH] + left + right
+        eps_out[0, f] = eps.astype(BF).reshape(TR, W, CH)
+        noisy = xv[f].reshape(TR * W, CH).astype(F32)
+        den_out[0, f] = (coefs[0, 0] * noisy - coefs[0, 1] * eps).astype(BF).reshape(TR, W, CH)
+
+    for upper in (True, False):
+
+        @pl.when(over_exists & (i == (0 if upper else 1)))
+        def _(upper=upper):
+            for k in range(8):
+                over_copy(k, upper).wait_send()
+
+
+def put_out(den, eps, den_out, eps_out, sems):
+    copies = [pltpu.make_async_copy(a, b, sems.at[q]) for q, (a, b) in enumerate(((den, den_out), (eps, eps_out)))]
+    for copy in copies:
+        copy.start()
+    for copy in copies:
+        copy.wait()
+
 
 def local(x, clip, picks, w_in, w_mid, proj, factors, w_up, w_dn, w_out, coefs):
+    args = (x, clip, picks, w_in, w_mid, proj, factors, w_up, w_dn, w_out, coefs)
+    args = [pltpu.with_memory_space_constraint(z, pltpu.HBM) for z in args]
     hbm = pl.BlockSpec(memory_space=pltpu.HBM)
+    vmem = pl.BlockSpec(memory_space=pltpu.VMEM)
     patch = pltpu.VMEM((8, 2, PR, PC, CH), BF)
     padded = pltpu.VMEM((PR + 2, PC + 2, NF, CH), BF)
-    side = pltpu.VMEM((4, PC + 2, NF, CH), BF)
-    upright = pltpu.VMEM((4, PR + 2, NF, CH), BF)
+    side = pltpu.VMEM((3, PC + 2, NF, CH), BF)
+    upright = pltpu.VMEM((3, PR + 2, NF, CH), BF)
     sums = pltpu.VMEM((PR, PC, NF, CH), F32)
     taps = pltpu.VMEM((3, 3, CH, CH), BF)
     dma = pltpu.SemaphoreType.DMA
-    eps = pl.pallas_call(
+    den, eps = pl.pallas_call(
         kernel,
-        out_shape=jax.ShapeDtypeStruct(x.shape, BF),
-        in_specs=[hbm] * 10,
-        out_specs=hbm,
+        out_shape=(pltpu.VMEM(x.shape, BF), pltpu.VMEM(x.shape, BF)),
+        in_specs=[hbm] * 11,
+        out_specs=(vmem, vmem),
         scratch_shapes=[
             pltpu.SMEM((1, 2), jnp.int32),
             pltpu.SMEM((1, 2), F32),
-            patch, patch, padded, padded, padded, padded, side, side, upright, upright, sums, sums,
+            pltpu.SMEM((1, 2), F32),
+            patch, patch, padded, padded, padded, side, side, upright, upright, sums, sums,
             pltpu.VMEM((8, NF, CH), F32),
             pltpu.VMEM((NF, PR, PC, CH), BF),
+            pltpu.VMEM((2, TR + 2, W, CH), BF),
+            pltpu.VMEM(x.shape[1:], BF),
             taps, taps, taps,
             pltpu.VMEM((CH, 3 * CH), BF),
             pltpu.VMEM((CH, CH), BF),
             pltpu.VMEM((CH, 4 * CH), BF),
             pltpu.VMEM((4 * CH, CH), BF),
-            taps,
-            dma((12,)), dma((8,)), dma((8,)), dma((8,)), dma((8,)), dma((8,)), dma((8,)),
-            dma((4, 8)), dma((4, 8)), dma((3, 8)), dma((3, 8)),
+            pltpu.VMEM((3, CH, 3 * CH), BF),
+            dma((16,)), dma((8,)), dma((8,)), dma((8,)), dma((8,)), dma((8,)), dma((8,)),
+            dma((3, 8)), dma((3, 8)), dma((3, 8)), dma((3, 8)), dma((8,)), dma((2, 4)),
         ],
         compiler_params=pltpu.CompilerParams(
-            collective_id=0, has_side_effects=True, vmem_limit_bytes=60 * 1024 * 1024
+            collective_id=0, has_side_effects=True, vmem_limit_bytes=32 * 1024 * 1024
         ),
         cost_estimate=pl.CostEstimate(flops=1_700_000_000, bytes_accessed=3_000_000, transcendentals=1_500_000),
         name="denoise",
-    )(x, clip, picks, w_in, w_mid, proj, factors, w_up, w_dn, w_out)
-    denoised = coefs[0, 0] * x.astype(F32) - coefs[0, 1] * eps.astype(F32)
-    return denoised.astype(BF), eps
+    )(*args)
+    outs = jax.ShapeDtypeStruct(x.shape, BF)
+    return pl.pallas_call(
+        put_out,
+        out_shape=(outs, outs),
+        in_specs=[vmem] * 2,
+        out_specs=(hbm, hbm),
+        scratch_shapes=[dma((2,))],
+        name="put_out",
+    )(*(pltpu.with_memory_space_constraint(z, pltpu.VMEM) for z in (den, eps)))
 
 
 def solution(mesh):

time: 51.5 us -> 43.3 us (0.84)
  other arithmetic: 3.13 us -> 0 us
  Pallas kernels: 45.4 us -> 42.5 us
  local copies, waits for them, and re-layouts: 2.1 us -> 0 us
    convert_element_type x1 -> x0, other arithmetic: 3.13 us -> none  [local(): return (denoised.astype(BF), eps)]
    pallas_call x1 -> x2, Pallas kernels: 45.4 us -> 42.5 us  [the longest x1 41.7 us: local(): pl.pallas_call(kernel, out_shape=(pltpu.VMEM(x.shape, BF), pltpu.VMEM(x.s...]
    slice x1 -> x0, local copies, waits for them, and re-layouts: 1.39 us -> none  [local(): denoised = coefs[0, 0] * x.astype(F32) - coefs[0, 1] * eps.astype(F32)]
    unnamed x5 -> x0, local copies, waits for them, and re-layouts: 0.71 us -> none
where the time goes in v3:
time: 43.3 us; the launch traced here: 43.1 us
  Pallas kernels  42.5 us (98%)
  between operations  0.64 us (1%)
    pallas_call x1, Pallas kernels, local(): pl.pallas_call(kernel, out_shape=(pltpu.VMEM(x.shape, BF), pltpu.VMEM(x.s...  41.7 us

profile of v3, /device:TPU:233, one launch (start us, length us, event | category | flops | bytes accessed | tf_op | source)
XLA Modules:
  0.0 43.1 jit_solution(10200311476332566538)
XLA Ops:
  0.6 41.7 %denoise.1 = (bf16[1,2,8,64,128]{4,3,2,1,0:T(8,128)(2,1)S(1)}, bf16[1,2,8,64,128]{4,3,2,1,0:T(8,128)(2,1)S(1)}) custom-call(bf16[1,2,8,64,128]{4,3,2,1,0:T(8,128)(2,1)} %x_hbm.1, bf16[1,2,8,64,128]{4,3,2,1,0:T(8,128)(2,1)} %clip_hbm.1, s32[1,2]{1,0:T(1,128)} %picks_hbm.1, bf16[1,3,3,256,128]{4,3,2,1,0:T(8,128)(2,1)} %w_in.1, ...), custom_call_target="tpu_custom_call" | custom-call | flops 1700000000 | bytes 3000000 | tf_op jit(solution)/shard_map/denoise/pallas_call | solution.py:432
  42.3 0.8 %put_out.1 = (bf16[1,2,8,64,128]{4,3,2,1,0:T(8,128)(2,1)}, bf16[1,2,8,64,128]{4,3,2,1,0:T(8,128)(2,1)}) custom-call(bf16[1,2,8,64,128]{4,3,2,1,0:T(8,128)(2,1)S(1)} %get-tuple-element.4.den, bf16[1,2,8,64,128]{4,3,2,1,0:T(8,128)(2,1)S(1)} %get-tuple-element.5.eps), custom_call_target="tpu_custom_call" | custom-call | tf_op jit(solution)/shard_map/put_out/pallas_call | solution.py:462

commit v4 on v3

v4 whole, which is shorter than its diff:
```python
import functools

import jax
import jax.numpy as jnp
from jax import lax
from jax.experimental import pallas as pl
from jax.experimental.pallas import tpu as pltpu
from jax.sharding import PartitionSpec as P

MESH = pl.DeviceIdType.MESH
BF = jnp.bfloat16
F32 = jnp.float32
PR, PC, NF, CH = 4, 16, 16, 128
TR, W = 8, 64
LONG = (0, 1)
DIRS = [(-1, 0), (1, 0), (0, -1), (0, 1), (-1, -1), (-1, 1), (1, -1), (1, 1)]
ROWS, COLS, CORNERS = (0, 1), (2, 3), (4, 5, 6, 7)


def dot(a, b):
    return jnp.dot(a, b, preferred_element_type=F32)


def lane_sums(v, ones):
    hi = v.astype(BF)
    lo = (v - hi.astype(F32)).astype(BF)
    return dot(jnp.concatenate([hi, lo], axis=1), jnp.concatenate([ones, ones], axis=0))


def silu(v):
    half = 0.5 * v
    return half + half * jnp.tanh(half)


def kernel(
    x_hbm, clip_hbm, picks_hbm, w_in, w_mid, proj, factors_hbm, w_up, w_dn, w_out,
    frames_c, xv, v_out,
    picks, factors, raw_n, raw_c, xn, xc, hb, top, bot, lef, rig, acc, res, pk, send_c, zeros, relayed,
    v_in, v_mid, v_proj, v_up, v_dn,
    s_w, s_pk, r_pk, s_c, r_c, s_l, r_n, s_n, s_h, r_h, s_e, r_e, s_o, r_o, s_z, r_l,
):
    s = lax.axis_index("segment")
    t = lax.axis_index("tile")
    d = lax.axis_index("frame")
    i, j = lax.rem(d, 2), lax.div(d, 2)
    big_row = 2 * t + i
    last_tile = lax.axis_size("tile") - 1
    last_row = 2 * last_tile + 1
    last_segment = lax.axis_size("segment") - 1

    def exists(dr, dc):
        row, col = big_row + dr, j + dc
        return (row >= 0) & (row <= last_row) & (col >= 0) & (col <= 3)

    def neighbour(dr, dc):
        row, col = big_row + dr, j + dc
        return {"tile": lax.div(row, 2), "frame": 2 * col + lax.rem(row, 2)}

    def in_group(k):
        return lax.rem(d + k, 8)

    y = 2 * s + lax.rem(t, 2)
    chips = 2 * (last_segment + 1)
    behind, ahead = lax.rem(y + chips - 3, chips), lax.rem(y + 3, chips)
    other_tile = t + 1 - 2 * lax.rem(t, 2)
    relays = (y >= chips - 3) | (y < chips - 5)

    def back_by_three(frame):
        return {"segment": lax.div(behind, 2), "tile": other_tile, "frame": frame}

    def wait_for(ref, sem):
        pltpu.make_async_copy(ref, ref, sem).wait()

    def signal(device):
        pl.semaphore_signal(barrier, inc=1, device_id=device, device_id_type=MESH)

    barrier = pltpu.get_barrier_semaphore()

    @pl.when(s > 0)
    def _():
        for k in range(8):
            if k not in LONG:
                signal({"segment": s - 1, "frame": lax.rem(d + 8 - k, 8)})
        for k in LONG[1:]:
            signal({"segment": lax.div(ahead, 2), "tile": other_tile, "frame": lax.rem(d + 8 - k, 8)})

    signal({"segment": lax.div(ahead, 2), "tile": other_tile})

    for ref in (top, bot, lef, rig):
        ref[...] = jnp.zeros(ref.shape, BF)

    for k in range(1, 8):
        signal({"frame": in_group(k)})

    @pl.when(t > 0)
    def _():
        for q in range(4):
            signal({"tile": t - 1, "frame": 2 * q + 1})

    @pl.when(t < last_tile)
    def _():
        for q in range(4):
            signal({"tile": t + 1, "frame": 2 * q})

    over = t + 2 * i - 1
    over_exists = (over >= 0) & (over <= last_tile)

    weights = [
        (picks_hbm, picks),
        (w_in.at[0], v_in),
        (factors_hbm, factors),
        (w_mid.at[0], v_mid),
        (proj.at[0], v_proj),
        (w_up.at[0], v_up),
        (w_dn.at[0], v_dn),
        (w_out.at[0], v_out),
        (x_hbm.at[0], xv),
    ]
    loads = [pltpu.make_async_copy(a, b, s_w.at[q]) for q, (a, b) in enumerate(weights)]
    for load in loads:
        load.start()
    for buf in (xn, xc, hb):
        buf[0] = jnp.zeros((PC + 2, NF, CH), BF)
        buf[PR + 1] = jnp.zeros((PC + 2, NF, CH), BF)
        buf[:, 0:1] = jnp.zeros((PR + 2, 1, NF, CH), BF)
        buf[:, PC + 1 : PC + 2] = jnp.zeros((PR + 2, 1, NF, CH), BF)
    zeros[...] = jnp.zeros(zeros.shape, BF)

    def no_row(to_row):
        return pltpu.make_async_copy(zeros, frames_c.at[:, to_row : to_row + 1], s_z)

    pl.when(t == 0)(lambda: no_row(0).start())
    pl.when(t == last_tile)(lambda: no_row(TR + 1).start())
    pl.semaphore_wait(barrier, 8 + jnp.where(relays, 1, 0) + jnp.where(s < last_segment, 6, 0) + jnp.where(over_exists, 8, 0))

    def patch_of(ref, c):
        return ref.at[0, :, pl.ds(PR * lax.rem(c, 2), PR), pl.ds(pl.multiple_of(PC * lax.div(c, 2), PC), PC), :]

    def clip_copy(k):
        return pltpu.make_async_remote_copy(
            src_ref=patch_of(clip_hbm, in_group(k)),
            dst_ref=raw_c.at[d],
            send_sem=s_c,
            recv_sem=r_c,
            device_id={"segment": s + 1, "frame": in_group(k)},
            device_id_type=MESH,
        )

    def first_half(q, k):
        return pltpu.make_async_remote_copy(
            src_ref=patch_of(clip_hbm, in_group(k)),
            dst_ref=relayed.at[q],
            send_sem=s_c,
            recv_sem=r_l.at[q],
            device_id=back_by_three(d),
            device_id_type=MESH,
        )

    def second_half(q, k):
        return pltpu.make_async_remote_copy(
            src_ref=relayed.at[q],
            dst_ref=raw_c.at[d],
            send_sem=s_l.at[q],
            recv_sem=r_c,
            device_id=back_by_three(in_group(k)),
            device_id_type=MESH,
        )

    @pl.when(s < last_segment)
    def _():
        for q, k in enumerate(LONG):
            first_half(q, k).start()
        for k in range(8):
            if k not in LONG:
                clip_copy(k).start()

    own_noisy = pltpu.make_async_copy(patch_of(x_hbm, d), raw_n.at[d], s_n.at[0])
    own_noisy.start()
    for k in range(1, 8):
        pltpu.make_async_remote_copy(
            src_ref=patch_of(x_hbm, in_group(k)),
            dst_ref=raw_n.at[d],
            send_sem=s_n.at[1],
            recv_sem=r_n,
            device_id={"frame": in_group(k)},
            device_id_type=MESH,
        ).start()
    loads[0].wait()
    frame_row = lax.broadcasted_iota(jnp.int32, (NF, CH), 0)
    pk[d] = jnp.where(frame_row == 2 * d, picks[0, 0], jnp.where(frame_row == 2 * d + 1, picks[0, 1], 0)).astype(F32)
    for k in range(1, 8):
        pltpu.make_async_remote_copy(
            src_ref=pk.at[d],
            dst_ref=pk.at[d],
            send_sem=s_pk,
            recv_sem=r_pk,
            device_id={"frame": in_group(k)},
            device_id_type=MESH,
        ).start()

    @pl.when(relays)
    def _():
        for q, k in enumerate(LONG):
            first_half(q, k).wait_recv()
            second_half(q, k).start()

    r_i = lax.broadcasted_iota(jnp.int32, (256, 256), 0)
    c_i = lax.broadcasted_iota(jnp.int32, (256, 256), 1)
    r_hi, r_lo, c_hi, c_lo = r_i // 16, r_i % 16, c_i // 16, c_i % 16
    swap = jnp.where((r_hi == c_lo) & (r_lo == c_hi), 1.0, 0.0).astype(BF)

    def halo_copy(buf, n, k):
        inner = slice(1, PC + 1)
        rows = slice(1, PR + 1)
        ends = [
            (buf.at[1, inner], bot.at[n, inner]),
            (buf.at[PR, inner], top.at[n, inner]),
            (buf.at[rows, 1], rig.at[n, rows]),
            (buf.at[rows, PC], lef.at[n, rows]),
            (buf.at[1, 1], bot.at[n, PC + 1]),
            (buf.at[1, PC], bot.at[n, 0]),
            (buf.at[PR, 1], top.at[n, PC + 1]),
            (buf.at[PR, PC], top.at[n, 0]),
        ]
        src, dst = ends[k]
        return pltpu.make_async_remote_copy(
            src_ref=src,
            dst_ref=dst,
            send_sem=s_h.at[k],
            recv_sem=r_h.at[n, k],
            device_id=neighbour(*DIRS[k]),
            device_id_type=MESH,
        )

    def halo_start(buf, n):
        for k in COLS + CORNERS + ROWS:
            pl.when(exists(*DIRS[k]))(halo_copy(buf, n, k).start)

    def halo_wait(buf, n, which):
        for k in which:
            dr, dc = DIRS[k]
            pl.when(exists(-dr, -dc))(halo_copy(buf, n, k).wait_recv)

    def halo_sent(buf, n):
        for k in range(8):
            pl.when(exists(*DIRS[k]))(halo_copy(buf, n, k).wait_send)

    def conv(buf, w, row, rows):
        n = rows * PC * NF
        parts = [
            buf[row + dr : row + dr + rows, dc : dc + PC].reshape(n, CH) for dr in range(3) for dc in range(3)
        ]
        return dot(jnp.concatenate(parts, axis=1), w.reshape(9 * CH, CH)).reshape(rows, PC, NF, CH)

    def add_rows(to, n, w):
        for row, ref, tap in ((0, top, 0), (PR - 1, bot, 2)):
            parts = [ref[n, dc : dc + PC].reshape(PC * NF, CH) for dc in range(3)]
            to[row] += dot(jnp.concatenate(parts, axis=1), w[tap].reshape(3 * CH, CH)).reshape(PC, NF, CH)

    def add_cols(to, n, w):
        for col, ref, tap in ((0, lef, 0), (PC - 1, rig, 2)):
            parts = [ref[n, dr : dr + PR].reshape(PR * NF, CH) for dr in range(3)]
            to[:, col] += dot(jnp.concatenate(parts, axis=1), w[:, tap].reshape(3 * CH, CH)).reshape(PR, NF, CH)

    own_noisy.wait()
    wait_for(raw_n.at[0:7], r_n)
    for row in range(PR):
        xn[row + 1, 1 : PC + 1] = dot(swap, raw_n[:, :, row].reshape(256, CH)).astype(BF).reshape(PC, NF, CH)
    halo_start(xn, 0)
    loads[1].wait()
    for row in (0, 2):
        acc[row : row + 2] = conv(xn, v_in[:, :, 0:CH, :], row, 2)

    wait_for(pk.at[0:7], r_pk)
    pick_rows = pk[0]
    for q in range(1, 8):
        pick_rows = pick_rows + pk[q]
    pick_rows = jnp.broadcast_to(pick_rows[None], (16, NF, CH)).reshape(256, CH)
    pick_rows = jnp.concatenate([pick_rows, pick_rows], axis=1)
    choose = jnp.where((r_hi == c_lo) & (pick_rows == c_hi.astype(F32)), 1.0, 0.0).astype(BF)

    @pl.when(s == 0)
    def _():
        raw_c[...] = jnp.zeros(raw_c.shape, BF)

    @pl.when(s > 0)
    def _():
        wait_for(raw_c, r_c)

    for row in range(PR):
        xc[row + 1, 1 : PC + 1] = dot(choose, raw_c[:, :, row].reshape(256, CH)).astype(BF).reshape(PC, NF, CH)
    halo_sent(xn, 0)
    halo_start(xc, 1)
    for load in loads[2:-2]:
        load.wait()
    for row in (0, 2):
        acc[row : row + 2] += conv(xc, v_in[:, :, CH : 2 * CH, :], row, 2)
    halo_wait(xn, 0, range(8))
    add_rows(acc, 0, v_in[:, :, 0:CH, :])
    add_cols(acc, 0, v_in[:, :, 0:CH, :])
    halo_wait(xc, 1, range(8))
    add_rows(acc, 1, v_in[:, :, CH : 2 * CH, :])
    add_cols(acc, 1, v_in[:, :, CH : 2 * CH, :])
    hb[1 : PR + 1, 1 : PC + 1] = silu(acc[...]).astype(BF)
    halo_sent(xc, 1)
    halo_start(hb, 2)

    lane_r = lax.broadcasted_iota(jnp.int32, (CH, CH), 0)
    lane_c = lax.broadcasted_iota(jnp.int32, (CH, CH), 1)
    ones = jnp.full((CH, CH), 1.0, BF)
    by_head = jnp.where(lane_r // 64 == lane_c // 64, 1.0, 0.0).astype(BF)
    first_head = lane_c < 64
    other_pixel = jnp.where(lane_r // 16 == lane_c // 16, 0.0, -1e30)
    for row in (0, 2):
        skip = hb[row + 1 : row + 3, 1 : PC + 1].astype(F32)
        res[row : row + 2] = skip + conv(hb, v_mid[...], row, 2)

    def two_rows(rows):
        a = jnp.concatenate([res[row].reshape(256, CH) for row in rows], axis=0)
        u = (a * lax.rsqrt(lane_sums(a * a, ones) * (1 / 128) + 1e-6)).astype(BF)
        qkv = dot(u, jnp.concatenate([v_proj[q] for q in range(3)], axis=1))
        q, k, v = qkv[:, 0:CH], qkv[:, CH : 2 * CH], qkv[:, 2 * CH : 3 * CH].astype(BF)
        qn = (q * lax.rsqrt(lane_sums(q * q, by_head) * (1 / 64) + 1e-6)).astype(BF)
        kn = (k * lax.rsqrt(lane_sums(k * k, by_head) * (1 / 64) + 1e-6)).astype(BF)
        parts = []
        zero = jnp.zeros((CH, CH), BF)
        for g in range(4):
            qg, kg, vg = (z[g * CH : (g + 1) * CH] for z in (qn, kn, v))
            both = jnp.concatenate([jnp.where(first_head, qg, zero), jnp.where(first_head, zero, qg)], axis=0)
            sc = lax.dot_general(both, kg, (((1,), (1,)), ((), ())), preferred_element_type=F32)
            sc = jnp.concatenate(
                [sc[h * CH : (h + 1) * CH] * (factors[0, h] * (1 / 64)) + other_pixel for h in range(2)], axis=0
            )
            e = jnp.exp(sc - jnp.max(sc, axis=1, keepdims=True))
            total = jnp.sum(e, axis=1, keepdims=True)
            o = dot(e.astype(BF), vg) / total
            parts.append(jnp.where(first_head, o[:CH], o[CH:]).astype(BF))
        b = a + dot(jnp.concatenate(parts, axis=0), v_proj[3])
        r = (b * lax.rsqrt(lane_sums(b * b, ones) * (1 / 128) + 1e-6)).astype(BF)
        m = silu(dot(r, v_up[...])).astype(BF)
        c = (b + dot(m, v_dn[...])).astype(BF)
        for q, row in enumerate(rows):
            part = dot(swap, c[q * 256 : (q + 1) * 256]).astype(BF)
            send_c[:, row] = part.reshape(NF, PC, CH)

    def give_back(first, size):
        to = frames_c.at[:, pl.ds(1 + PR * i + first, size), pl.ds(pl.multiple_of(PC * j, PC), PC), :]
        for k in range(1, 8):
            pltpu.make_async_remote_copy(
                src_ref=send_c.at[pl.ds(2 * in_group(k), 2), first : first + size],
                dst_ref=to,
                send_sem=s_e.at[0],
                recv_sem=r_e,
                device_id={"frame": in_group(k)},
                device_id_type=MESH,
            ).start()
        pltpu.make_async_copy(send_c.at[pl.ds(2 * d, 2), first : first + size], to, s_e.at[1]).start()

    halo_wait(hb, 2, COLS)
    add_cols(res, 2, v_mid[...])
    halo_wait(hb, 2, ROWS + CORNERS)
    add_rows(res, 2, v_mid[...])
    two_rows((0, 3))

    def over_copy(k, upper):
        first, to_row = (0, TR + 1) if upper else (PR - 1, 0)
        device = {"tile": over, "frame": in_group(k)}
        src = send_c.at[pl.ds(2 * in_group(k), 2), first : first + 1]
        dst = frames_c.at[:, to_row : to_row + 1, pl.ds(pl.multiple_of(PC * j, PC), PC), :]
        return pltpu.make_async_remote_copy(
            src_ref=src,
            dst_ref=dst,
            send_sem=s_o,
            recv_sem=r_o.at[1 if upper else 0],
            device_id=device,
            device_id_type=MESH,
        )

    for upper in (True, False):

        @pl.when(over_exists & (i == (0 if upper else 1)))
        def _(upper=upper):
            for k in range(8):
                over_copy(k, upper).start()

    give_back(0, 1)
    give_back(PR - 1, 1)
    two_rows((1, 2))
    give_back(1, 2)
    halo_sent(hb, 2)
    wait_for(pk.at[0:7], s_pk)
    wait_for(raw_n.at[0:7], s_n.at[1])

    @pl.when(s < last_segment)
    def _():
        wait_for(raw_c, s_c)

    @pl.when(relays)
    def _():
        for q, k in enumerate(LONG):
            second_half(q, k).wait_send()

    pl.when(t == 0)(lambda: no_row(0).wait())
    pl.when(t == last_tile)(lambda: no_row(TR + 1).wait())
    loads[-2].wait()
    loads[-1].wait()
    wait_for(raw_n.at[0:7], s_e.at[0])
    pl.when(over_exists)(lambda: wait_for(send_c.at[:, 0:1], s_o))
    wait_for(raw_n.at[0], s_e.at[1])
    wait_for(raw_n.at[0:7], r_e)
    pl.when(t > 0)(lambda: wait_for(frames_c.at[:, 0:1], r_o.at[0]))
    pl.when(t < last_tile)(lambda: wait_for(frames_c.at[:, TR + 1 : TR + 2], r_o.at[1]))


def last_conv(frames_c, xv, v_out, coefs_hbm, den_out, eps_out, coefs, den, eps, s_in, s_den, s_eps):
    load = pltpu.make_async_copy(coefs_hbm, coefs, s_in)
    load.start()
    column = lax.rem(lax.broadcasted_iota(jnp.int32, (TR * W, CH), 0), W)
    taps = jnp.concatenate([v_out[:, q].reshape(3 * CH, CH) for q in range(3)], axis=1)
    copies = []
    for f in range(2):
        rows = [frames_c[f, dr : dr + TR].reshape(TR * W, CH) for dr in range(3)]
        out = dot(jnp.concatenate(rows, axis=1), taps)
        left = jnp.where(column == 0, 0.0, pltpu.roll(out[:, 0:CH], 1, 0))
        right = jnp.where(column == W - 1, 0.0, pltpu.roll(out[:, 2 * CH :], TR * W - 1, 0))
        total = out[:, CH : 2 * CH] + left + right
        eps[f] = total.astype(BF).reshape(TR, W, CH)
        if f == 0:
            load.wait()
        noisy = xv[f].reshape(TR * W, CH).astype(F32)
        den[f] = (coefs[0, 0] * noisy - coefs[0, 1] * total).astype(BF).reshape(TR, W, CH)
        copies.append(pltpu.make_async_copy(eps.at[f], eps_out.at[0, f], s_eps.at[f]))
        copies.append(pltpu.make_async_copy(den.at[f], den_out.at[0, f], s_den.at[f]))
        copies[-2].start()
        copies[-1].start()
    for copy in copies:
        copy.wait()


def local(x, clip, picks, w_in, w_mid, proj, factors, w_up, w_dn, w_out, coefs):
    args = (x, clip, picks, w_in, w_mid, proj, factors, w_up, w_dn, w_out, coefs)
    args = [pltpu.with_memory_space_constraint(z, pltpu.HBM) for z in args]
    hbm = pl.BlockSpec(memory_space=pltpu.HBM)
    vmem = pl.BlockSpec(memory_space=pltpu.VMEM)
    patch = pltpu.VMEM((8, 2, PR, PC, CH), BF)
    padded = pltpu.VMEM((PR + 2, PC + 2, NF, CH), BF)
    side = pltpu.VMEM((3, PC + 2, NF, CH), BF)
    upright = pltpu.VMEM((3, PR + 2, NF, CH), BF)
    sums = pltpu.VMEM((PR, PC, NF, CH), F32)
    taps = pltpu.VMEM((3, 3, CH, CH), BF)
    dma = pltpu.SemaphoreType.DMA
    frames_c, xv, v_out = pl.pallas_call(
        kernel,
        out_shape=(
            pltpu.VMEM((2, TR + 2, W, CH), BF),
            pltpu.VMEM(x.shape[1:], BF),
            pltpu.VMEM((3, 3, CH, CH), BF),
        ),
        in_specs=[hbm] * 10,
        out_specs=[pl.BlockSpec(memory_space=pl.ANY)] * 3,
        scratch_shapes=[
            pltpu.SMEM((1, 2), jnp.int32),
            pltpu.SMEM((1, 2), F32),
            patch, patch, padded, padded, padded, side, side, upright, upright, sums, sums,
            pltpu.VMEM((8, NF, CH), F32),
            pltpu.VMEM((NF, PR, PC, CH), BF),
            pltpu.VMEM((2, 1, W, CH), BF),
            pltpu.VMEM((2, 2, PR, PC, CH), BF),
            pltpu.VMEM((3, 3, 2 * CH, CH), BF),
            taps,
            pltpu.VMEM((4, CH, CH), BF),
            pltpu.VMEM((CH, 4 * CH), BF),
            pltpu.VMEM((4 * CH, CH), BF),
            dma((9,)), dma, dma, dma, dma, dma((2,)), dma, dma((2,)),
            dma((8,)), dma((3, 8)), dma((2,)), dma, dma, dma((2,)), dma, dma((2,)),
        ],
        compiler_params=pltpu.CompilerParams(
            collective_id=0, has_side_effects=True, vmem_limit_bytes=32 * 1024 * 1024
        ),
        cost_estimate=pl.CostEstimate(flops=1_700_000_000, bytes_accessed=3_000_000, transcendentals=1_500_000),
        name="denoise",
    )(*args[:10])
    outs = jax.ShapeDtypeStruct(x.shape, BF)
    in_vmem = [pltpu.with_memory_space_constraint(z, pltpu.VMEM) for z in (frames_c, xv, v_out)]
    frames = pltpu.VMEM(x.shape[1:], BF)
    return pl.pallas_call(
        last_conv,
        out_shape=(outs, outs),
        in_specs=[vmem, vmem, vmem, hbm],
        out_specs=(hbm, hbm),
        scratch_shapes=[pltpu.SMEM((1, 2), F32), frames, frames, dma, dma((2,)), dma((2,))],
        compiler_params=pltpu.CompilerParams(vmem_limit_bytes=16 * 1024 * 1024),
        name="last_conv",
    )(*in_vmem, args[10])


def solution(mesh):
    clip = P("segment", "frame", "tile", None, None)
    kernel_spec = P("segment", None, None, None, None)
    in_specs = (
        clip, clip, P("segment", "frame"), kernel_spec, kernel_spec, P("segment", None, None, None),
        P("segment", None), P("segment", None, None), P("segment", None, None), kernel_spec, P("segment", None),
    )
    return jax.shard_map(local, mesh=mesh, in_specs=in_specs, out_specs=(clip, clip), check_vma=False)
```

time: 43.3 us -> 40.2 us (0.928)
  the two profiles are of different devices: /device:TPU:233 before, /device:TPU:217 now
where the time goes in v4:
time: 40.2 us; the launch traced here: 40 us
  Pallas kernels  39.4 us (98%)
  between operations  0.64 us (2%)
    pallas_call x1, Pallas kernels, local(): pl.pallas_call(kernel, out_shape=(pltpu.VMEM((2, TR + 2, W, CH), BF), plt...  37.5 us
    pallas_call x1, Pallas kernels, local(): pl.pallas_call(last_conv, out_shape=(outs, outs), in_specs=[vmem, vmem, v...  1.86 us

profile of v4, /device:TPU:217, one launch (start us, length us, event | category | flops | bytes accessed | tf_op | source)
XLA Modules:
  0.0 40.0 jit_solution(12753038498907306203)
XLA Ops:
  0.6 37.5 %denoise.1 = (bf16[2,10,64,128]{3,2,1,0:T(8,128)(2,1)S(1)}, bf16[2,8,64,128]{3,2,1,0:T(8,128)(2,1)S(1)}, bf16[3,3,128,128]{3,2,1,0:T(8,128)(2,1)S(1)}) custom-call(bf16[1,2,8,64,128]{4,3,2,1,0:T(8,128)(2,1)} %x_hbm.1, bf16[1,2,8,64,128]{4,3,2,1,0:T(8,128)(2,1)} %clip_hbm.1, s32[1,2]{1,0:T(1,128)} %picks_hbm.1, bf16[1,3,3,256,128]{4,3,2,1,0:T(8,128)(2,1)} %w_in.1, ...), custom_call_target="tpu_custom_call" | custom-call | flops 1700000000 | bytes 3000000 | tf_op jit(solution)/shard_map/denoise/pallas_call | solution.py:452
  38.2 1.9 %last_conv.1 = (bf16[1,2,8,64,128]{4,3,2,1,0:T(8,128)(2,1)}, bf16[1,2,8,64,128]{4,3,2,1,0:T(8,128)(2,1)}) custom-call(bf16[2,10,64,128]{3,2,1,0:T(8,128)(2,1)S(1)} %get-tuple-element.5.frames_c, bf16[2,8,64,128]{3,2,1,0:T(8,128)(2,1)S(1)} %get-tuple-element.6.xv, bf16[3,3,128,128]{3,2,1,0:T(8,128)(2,1)S(1)} %get-tuple-element.7.v_out, f32[1,2]{1,0:T(1,128)} %coefs_hbm.1), custom_call_target="tpu_custom_call" | custom-call | tf_op jit(solution)/shard_map/last_conv/pallas_call | solution.py:486

commit v5 on v4

--- a/solution.py
+++ b/solution.py
@@ -33,9 +33,9 @@
 
 
 def kernel(
-    x_hbm, clip_hbm, picks_hbm, w_in, w_mid, proj, factors_hbm, w_up, w_dn, w_out,
-    frames_c, xv, v_out,
-    picks, factors, raw_n, raw_c, xn, xc, hb, top, bot, lef, rig, acc, res, pk, send_c, zeros, relayed,
+    x_hbm, clip_hbm, picks_hbm, w_in, w_mid, proj, factors_hbm, w_up, w_dn, w_out, coefs_hbm,
+    frames_c, xv, v_out, coef_rows,
+    picks, factors, coefs, coef_block, raw_n, raw_c, xn, xc, hb, top, bot, lef, rig, acc, res, pk, send_c, zeros, relayed,
     v_in, v_mid, v_proj, v_up, v_dn,
     s_w, s_pk, r_pk, s_c, r_c, s_l, r_n, s_n, s_h, r_h, s_e, r_e, s_o, r_o, s_z, r_l,
 ):
@@ -65,6 +65,11 @@
     other_tile = t + 1 - 2 * lax.rem(t, 2)
     relays = (y >= chips - 3) | (y < chips - 5)
 
+    def both_round(source):
+        return (source != 0) & (source != 3)
+
+    last_source = lax.rem(y + chips - 2, chips)
+
     def back_by_three(frame):
         return {"segment": lax.div(behind, 2), "tile": other_tile, "frame": frame}
 
@@ -81,8 +86,15 @@
         for k in range(8):
             if k not in LONG:
                 signal({"segment": s - 1, "frame": lax.rem(d + 8 - k, 8)})
-        for k in LONG[1:]:
-            signal({"segment": lax.div(ahead, 2), "tile": other_tile, "frame": lax.rem(d + 8 - k, 8)})
+        sender = lax.rem(d + 8 - LONG[1], 8)
+
+        @pl.when(both_round(last_source))
+        def _():
+            signal({"segment": lax.div(ahead, 2), "tile": other_tile, "frame": sender})
+
+        @pl.when(jnp.logical_not(both_round(last_source)))
+        def _():
+            signal({"segment": s - 1, "frame": sender})
 
     signal({"segment": lax.div(ahead, 2), "tile": other_tile})
 
@@ -109,6 +121,7 @@
         (picks_hbm, picks),
         (w_in.at[0], v_in),
         (factors_hbm, factors),
+        (coefs_hbm, coefs),
         (w_mid.at[0], v_mid),
         (proj.at[0], v_proj),
         (w_up.at[0], v_up),
@@ -127,11 +140,11 @@
     zeros[...] = jnp.zeros(zeros.shape, BF)
 
     def no_row(to_row):
-        return pltpu.make_async_copy(zeros, frames_c.at[:, to_row : to_row + 1], s_z)
+        return pltpu.make_async_copy(zeros, frames_c.at[:, to_row : to_row + 1], s_z.at[0])
 
     pl.when(t == 0)(lambda: no_row(0).start())
     pl.when(t == last_tile)(lambda: no_row(TR + 1).start())
-    pl.semaphore_wait(barrier, 8 + jnp.where(relays, 1, 0) + jnp.where(s < last_segment, 6, 0) + jnp.where(over_exists, 8, 0))
+    pl.semaphore_wait(barrier, 8 + jnp.where(relays & both_round(ahead), 1, 0) + jnp.where(s < last_segment, jnp.where(both_round(y), 6, 7), 0) + jnp.where(over_exists, 8, 0))
 
     def patch_of(ref, c):
         return ref.at[0, :, pl.ds(PR * lax.rem(c, 2), PR), pl.ds(pl.multiple_of(PC * lax.div(c, 2), PC), PC), :]
@@ -168,8 +181,9 @@
 
     @pl.when(s < last_segment)
     def _():
-        for q, k in enumerate(LONG):
-            first_half(q, k).start()
+        first_half(0, LONG[0]).start()
+        pl.when(both_round(y))(lambda: first_half(1, LONG[1]).start())
+        pl.when(jnp.logical_not(both_round(y)))(lambda: clip_copy(LONG[1]).start())
         for k in range(8):
             if k not in LONG:
                 clip_copy(k).start()
@@ -198,9 +212,10 @@
             device_id_type=MESH,
         ).start()
 
-    @pl.when(relays)
-    def _():
-        for q, k in enumerate(LONG):
+    for q, k in enumerate(LONG):
+
+        @pl.when(relays if q == 0 else relays & both_round(ahead))
+        def _(q=q, k=k):
             first_half(q, k).wait_recv()
             second_half(q, k).start()
 
@@ -226,7 +241,7 @@
         return pltpu.make_async_remote_copy(
             src_ref=src,
             dst_ref=dst,
-            send_sem=s_h.at[k],
+            send_sem=s_h.at[n % 2, k],
             recv_sem=r_h.at[n, k],
             device_id=neighbour(*DIRS[k]),
             device_id_type=MESH,
@@ -289,10 +304,13 @@
 
     for row in range(PR):
         xc[row + 1, 1 : PC + 1] = dot(choose, raw_c[:, :, row].reshape(256, CH)).astype(BF).reshape(PC, NF, CH)
-    halo_sent(xn, 0)
     halo_start(xc, 1)
     for load in loads[2:-2]:
         load.wait()
+    half_row = lax.broadcasted_iota(jnp.int32, (8, CH), 0) < 4
+    coef_block[...] = jnp.where(half_row, coefs[0, 0], coefs[0, 1])
+    coef_copy = pltpu.make_async_copy(coef_block, coef_rows, s_z.at[1])
+    coef_copy.start()
     for row in (0, 2):
         acc[row : row + 2] += conv(xc, v_in[:, :, CH : 2 * CH, :], row, 2)
     halo_wait(xn, 0, range(8))
@@ -302,7 +320,7 @@
     add_rows(acc, 1, v_in[:, :, CH : 2 * CH, :])
     add_cols(acc, 1, v_in[:, :, CH : 2 * CH, :])
     hb[1 : PR + 1, 1 : PC + 1] = silu(acc[...]).astype(BF)
-    halo_sent(xc, 1)
+    halo_sent(xn, 0)
     halo_start(hb, 2)
 
     lane_r = lax.broadcasted_iota(jnp.int32, (CH, CH), 0)
@@ -317,7 +335,7 @@
 
     def two_rows(rows):
         a = jnp.concatenate([res[row].reshape(256, CH) for row in rows], axis=0)
-        u = (a * lax.rsqrt(lane_sums(a * a, ones) * (1 / 128) + 1e-6)).astype(BF)
+        u = (a * lax.rsqrt(jnp.mean(a * a, axis=1, keepdims=True) + 1e-6)).astype(BF)
         qkv = dot(u, jnp.concatenate([v_proj[q] for q in range(3)], axis=1))
         q, k, v = qkv[:, 0:CH], qkv[:, CH : 2 * CH], qkv[:, 2 * CH : 3 * CH].astype(BF)
         qn = (q * lax.rsqrt(lane_sums(q * q, by_head) * (1 / 64) + 1e-6)).astype(BF)
@@ -333,10 +351,11 @@
             )
             e = jnp.exp(sc - jnp.max(sc, axis=1, keepdims=True))
             total = jnp.sum(e, axis=1, keepdims=True)
-            o = dot(e.astype(BF), vg) / total
-            parts.append(jnp.where(first_head, o[:CH], o[CH:]).astype(BF))
+            o = dot(e.astype(BF), vg)
+            total = jnp.where(first_head, total[:CH], total[CH:])
+            parts.append((jnp.where(first_head, o[:CH], o[CH:]) / total).astype(BF))
         b = a + dot(jnp.concatenate(parts, axis=0), v_proj[3])
-        r = (b * lax.rsqrt(lane_sums(b * b, ones) * (1 / 128) + 1e-6)).astype(BF)
+        r = (b * lax.rsqrt(jnp.mean(b * b, axis=1, keepdims=True) + 1e-6)).astype(BF)
         m = silu(dot(r, v_up[...])).astype(BF)
         c = (b + dot(m, v_dn[...])).astype(BF)
         for q, row in enumerate(rows):
@@ -387,6 +406,7 @@
     give_back(PR - 1, 1)
     two_rows((1, 2))
     give_back(1, 2)
+    halo_sent(xc, 1)
     halo_sent(hb, 2)
     wait_for(pk.at[0:7], s_pk)
     wait_for(raw_n.at[0:7], s_n.at[1])
@@ -395,13 +415,15 @@
     def _():
         wait_for(raw_c, s_c)
 
-    @pl.when(relays)
-    def _():
-        for q, k in enumerate(LONG):
+    for q, k in enumerate(LONG):
+
+        @pl.when(relays if q == 0 else relays & both_round(ahead))
+        def _(q=q, k=k):
             second_half(q, k).wait_send()
 
     pl.when(t == 0)(lambda: no_row(0).wait())
     pl.when(t == last_tile)(lambda: no_row(TR + 1).wait())
+    coef_copy.wait()
     loads[-2].wait()
     loads[-1].wait()
     wait_for(raw_n.at[0:7], s_e.at[0])
@@ -412,9 +434,7 @@
     pl.when(t < last_tile)(lambda: wait_for(frames_c.at[:, TR + 1 : TR + 2], r_o.at[1]))
 
 
-def last_conv(frames_c, xv, v_out, coefs_hbm, den_out, eps_out, coefs, den, eps, s_in, s_den, s_eps):
-    load = pltpu.make_async_copy(coefs_hbm, coefs, s_in)
-    load.start()
+def last_conv(frames_c, xv, v_out, coef_rows, den_out, eps_out, den, eps, s_den, s_eps):
     column = lax.rem(lax.broadcasted_iota(jnp.int32, (TR * W, CH), 0), W)
     taps = jnp.concatenate([v_out[:, q].reshape(3 * CH, CH) for q in range(3)], axis=1)
     copies = []
@@ -425,13 +445,11 @@
         right = jnp.where(column == W - 1, 0.0, pltpu.roll(out[:, 2 * CH :], TR * W - 1, 0))
         total = out[:, CH : 2 * CH] + left + right
         eps[f] = total.astype(BF).reshape(TR, W, CH)
-        if f == 0:
-            load.wait()
+        copies.append(pltpu.make_async_copy(eps.at[f], eps_out.at[0, f], s_eps.at[f]))
+        copies[-1].start()
         noisy = xv[f].reshape(TR * W, CH).astype(F32)
-        den[f] = (coefs[0, 0] * noisy - coefs[0, 1] * total).astype(BF).reshape(TR, W, CH)
-        copies.append(pltpu.make_async_copy(eps.at[f], eps_out.at[0, f], s_eps.at[f]))
+        den[f] = (coef_rows[0:1] * noisy - coef_rows[4:5] * total).astype(BF).reshape(TR, W, CH)
         copies.append(pltpu.make_async_copy(den.at[f], den_out.at[0, f], s_den.at[f]))
-        copies[-2].start()
         copies[-1].start()
     for copy in copies:
         copy.wait()
@@ -449,18 +467,21 @@
     sums = pltpu.VMEM((PR, PC, NF, CH), F32)
     taps = pltpu.VMEM((3, 3, CH, CH), BF)
     dma = pltpu.SemaphoreType.DMA
-    frames_c, xv, v_out = pl.pallas_call(
+    frames_c, xv, v_out, coef_rows = pl.pallas_call(
         kernel,
         out_shape=(
             pltpu.VMEM((2, TR + 2, W, CH), BF),
             pltpu.VMEM(x.shape[1:], BF),
             pltpu.VMEM((3, 3, CH, CH), BF),
+            pltpu.VMEM((8, CH), F32),
         ),
-        in_specs=[hbm] * 10,
-        out_specs=[pl.BlockSpec(memory_space=pl.ANY)] * 3,
+        in_specs=[hbm] * 11,
+        out_specs=[pl.BlockSpec(memory_space=pl.ANY)] * 4,
         scratch_shapes=[
             pltpu.SMEM((1, 2), jnp.int32),
             pltpu.SMEM((1, 2), F32),
+            pltpu.SMEM((1, 2), F32),
+            pltpu.VMEM((8, CH), F32),
             patch, patch, padded, padded, padded, side, side, upright, upright, sums, sums,
             pltpu.VMEM((8, NF, CH), F32),
             pltpu.VMEM((NF, PR, PC, CH), BF),
@@ -471,27 +492,27 @@
             pltpu.VMEM((4, CH, CH), BF),
             pltpu.VMEM((CH, 4 * CH), BF),
             pltpu.VMEM((4 * CH, CH), BF),
-            dma((9,)), dma, dma, dma, dma, dma((2,)), dma, dma((2,)),
-            dma((8,)), dma((3, 8)), dma((2,)), dma, dma, dma((2,)), dma, dma((2,)),
+            dma((10,)), dma, dma, dma, dma, dma((2,)), dma, dma((2,)),
+            dma((2, 8)), dma((3, 8)), dma((2,)), dma, dma, dma((2,)), dma((2,)), dma((2,)),
         ],
         compiler_params=pltpu.CompilerParams(
             collective_id=0, has_side_effects=True, vmem_limit_bytes=32 * 1024 * 1024
         ),
         cost_estimate=pl.CostEstimate(flops=1_700_000_000, bytes_accessed=3_000_000, transcendentals=1_500_000),
         name="denoise",
-    )(*args[:10])
+    )(*args)
     outs = jax.ShapeDtypeStruct(x.shape, BF)
-    in_vmem = [pltpu.with_memory_space_constraint(z, pltpu.VMEM) for z in (frames_c, xv, v_out)]
+    in_vmem = [pltpu.with_memory_space_constraint(z, pltpu.VMEM) for z in (frames_c, xv, v_out, coef_rows)]
     frames = pltpu.VMEM(x.shape[1:], BF)
     return pl.pallas_call(
         last_conv,
         out_shape=(outs, outs),
-        in_specs=[vmem, vmem, vmem, hbm],
+        in_specs=[vmem] * 4,
         out_specs=(hbm, hbm),
-        scratch_shapes=[pltpu.SMEM((1, 2), F32), frames, frames, dma, dma((2,)), dma((2,))],
+        scratch_shapes=[frames, frames, dma((2,)), dma((2,))],
         compiler_params=pltpu.CompilerParams(vmem_limit_bytes=16 * 1024 * 1024),
         name="last_conv",
-    )(*in_vmem, args[10])
+    )(*in_vmem)
 
 
 def solution(mesh):

time: 40.2 us -> 38.2 us (0.950)
  the two profiles are of different devices: /device:TPU:217 before, /device:TPU:233 now
where the time goes in v5:
time: 38.2 us; the launch traced here: 38 us
  Pallas kernels  37.4 us (98%)
  between operations  0.64 us (2%)
    pallas_call x1, Pallas kernels, local(): pl.pallas_call(kernel, out_shape=(pltpu.VMEM((2, TR + 2, W, CH), BF), plt...  36 us
    pallas_call x1, Pallas kernels, local(): pl.pallas_call(last_conv, out_shape=(outs, outs), in_specs=[vmem] * 4, ou...  1.39 us

profile of v5, /device:TPU:233, one launch (start us, length us, event | category | flops | bytes accessed | tf_op | source)
XLA Modules:
  0.0 38.0 jit_solution(12229260420928464557)
XLA Ops:
  0.6 36.0 %denoise.1 = (bf16[2,10,64,128]{3,2,1,0:T(8,128)(2,1)S(1)}, bf16[2,8,64,128]{3,2,1,0:T(8,128)(2,1)S(1)}, bf16[3,3,128,128]{3,2,1,0:T(8,128)(2,1)S(1)}, f32[8,128]{1,0:T(8,128)S(1)}) custom-call(bf16[1,2,8,64,128]{4,3,2,1,0:T(8,128)(2,1)} %x_hbm.1, bf16[1,2,8,64,128]{4,3,2,1,0:T(8,128)(2,1)} %clip_hbm.1, s32[1,2]{1,0:T(1,128)} %picks_hbm.1, ...), custom_call_target="tpu_custom_call" | custom-call | flops 1700000000 | bytes 3000000 | tf_op jit(solution)/shard_map/denoise/pallas_call | solution.py:470
  36.6 1.4 %last_conv.1 = (bf16[1,2,8,64,128]{4,3,2,1,0:T(8,128)(2,1)}, bf16[1,2,8,64,128]{4,3,2,1,0:T(8,128)(2,1)}) custom-call(bf16[2,10,64,128]{3,2,1,0:T(8,128)(2,1)S(1)} %get-tuple-element.6.frames_c, bf16[2,8,64,128]{3,2,1,0:T(8,128)(2,1)S(1)} %get-tuple-element.7.xv, bf16[3,3,128,128]{3,2,1,0:T(8,128)(2,1)S(1)} %get-tuple-element.8.v_out, ...), custom_call_target="tpu_custom_call" | custom-call | tf_op jit(solution)/shard_map/last_conv/pallas_call | solution.py:507

commit v6 on v5

--- a/solution.py
+++ b/solution.py
@@ -248,8 +248,11 @@
         )
 
     def halo_start(buf, n):
-        for k in COLS + CORNERS + ROWS:
+        for k in COLS + CORNERS:
             pl.when(exists(*DIRS[k]))(halo_copy(buf, n, k).start)
+        pl.when(exists(*DIRS[0]) & (i == 0))(halo_copy(buf, n, 0).start)
+        pl.when(exists(*DIRS[1]))(halo_copy(buf, n, 1).start)
+        pl.when(exists(*DIRS[0]) & (i == 1))(halo_copy(buf, n, 0).start)
 
     def halo_wait(buf, n, which):
         for k in which:
@@ -316,9 +319,10 @@
     halo_wait(xn, 0, range(8))
     add_rows(acc, 0, v_in[:, :, 0:CH, :])
     add_cols(acc, 0, v_in[:, :, 0:CH, :])
-    halo_wait(xc, 1, range(8))
+    halo_wait(xc, 1, COLS)
+    add_cols(acc, 1, v_in[:, :, CH : 2 * CH, :])
+    halo_wait(xc, 1, ROWS + CORNERS)
     add_rows(acc, 1, v_in[:, :, CH : 2 * CH, :])
-    add_cols(acc, 1, v_in[:, :, CH : 2 * CH, :])
     hb[1 : PR + 1, 1 : PC + 1] = silu(acc[...]).astype(BF)
     halo_sent(xn, 0)
     halo_start(hb, 2)

time: 38.2 us -> 38.2 us (level)
  no operation moved by 1% of the time
where the time goes in v6:
time: 38.2 us; the launch traced here: 38 us
  Pallas kernels  37.4 us (98%)
  between operations  0.64 us (2%)
    pallas_call x1, Pallas kernels, local(): pl.pallas_call(kernel, out_shape=(pltpu.VMEM((2, TR + 2, W, CH), BF), plt...  36 us
    pallas_call x1, Pallas kernels, local(): pl.pallas_call(last_conv, out_shape=(outs, outs), in_specs=[vmem] * 4, ou...  1.39 us

profile of v6, /device:TPU:233, one launch (start us, length us, event | category | flops | bytes accessed | tf_op | source)
XLA Modules:
  0.0 38.0 jit_solution(6935818306833093767)
XLA Ops:
  0.6 36.0 %denoise.1 = (bf16[2,10,64,128]{3,2,1,0:T(8,128)(2,1)S(1)}, bf16[2,8,64,128]{3,2,1,0:T(8,128)(2,1)S(1)}, bf16[3,3,128,128]{3,2,1,0:T(8,128)(2,1)S(1)}, f32[8,128]{1,0:T(8,128)S(1)}) custom-call(bf16[1,2,8,64,128]{4,3,2,1,0:T(8,128)(2,1)} %x_hbm.1, bf16[1,2,8,64,128]{4,3,2,1,0:T(8,128)(2,1)} %clip_hbm.1, s32[1,2]{1,0:T(1,128)} %picks_hbm.1, ...), custom_call_target="tpu_custom_call" | custom-call | flops 1700000000 | bytes 3000000 | tf_op jit(solution)/shard_map/denoise/pallas_call | solution.py:474
  36.6 1.4 %last_conv.1 = (bf16[1,2,8,64,128]{4,3,2,1,0:T(8,128)(2,1)}, bf16[1,2,8,64,128]{4,3,2,1,0:T(8,128)(2,1)}) custom-call(bf16[2,10,64,128]{3,2,1,0:T(8,128)(2,1)S(1)} %get-tuple-element.6.frames_c, bf16[2,8,64,128]{3,2,1,0:T(8,128)(2,1)S(1)} %get-tuple-element.7.xv, bf16[3,3,128,128]{3,2,1,0:T(8,128)(2,1)S(1)} %get-tuple-element.8.v_out, ...), custom_call_target="tpu_custom_call" | custom-call | tf_op jit(solution)/shard_map/last_conv/pallas_call | solution.py:511
